TPU v7x, 32 devices: a whole 2x2x4 slice. The times are simulated.
32 devices in a mesh: gx: 4 (over z), gy: 8 (over y, x, core).
Axes of the slice: x: 2, y: 2, z: 4, core: 2. Of those that a mesh axis runs over, the one named last changes fastest.
Arguments:
- leaf_maps: float32 [4, 8, 512, 512], P('gx', 'gy'), may hold values from -8 to 20, as said below
- leaf_fluxes: float32 [4, 8, 512, 128], P('gx', 'gy'), may hold values from -24 to 24
Outputs:
- boundary_values: float32 [4, 8, 512, 128], P('gx', 'gy')
Inputs may be any that keep to these rules, and one draw needn't show every extreme that they name: `leaf_maps`: every leaf's map is symmetric and positive definite with smallest eigenvalue 0.1 or more.
All inputs are finite; a program needn't handle non-finite values.
Results may differ from a plain program's by a relative error of at most 0.0003.
Values sent between devices are 32-bit elements; how exact they have to be, the bound alone decides.
A program may use at most 128 MiB of HBM per device.

v0:
```python
import jax
import jax.numpy as jnp
from jax import lax
from jax.sharding import PartitionSpec as P

LEVELS = 4


side_names = ("left", "right", "bottom", "top")


def from_partner(block, axis, stride):
    count = lax.axis_size(axis)
    route = []
    for low in range(count):
        high = low | 1 << stride
        if high != low and high < count:
            route += [(low, high), (high, low)]
    return lax.ppermute(block, axis, route)


def side_spans(cols_count, rows_count, patch_side):
    lengths = {
        "left": rows_count * patch_side,
        "right": rows_count * patch_side,
        "bottom": cols_count * patch_side,
        "top": cols_count * patch_side,
    }
    starts = {}
    running = 0
    for side_name in side_names:
        starts[side_name] = running
        running = running + lengths[side_name]
    return (starts, lengths)


def merge_layout(direction):
    if direction == "y":
        return (
            ("top", "bottom"),
            ((0, "left"), (1, "left"), (0, "right"), (1, "right"), (0, "bottom"), (1, "top")),
        )
    return (
        ("right", "left"),
        ((0, "left"), (1, "right"), (0, "bottom"), (1, "bottom"), (0, "top"), (1, "top")),
    )


def level_plan(levels):
    merge_plan = []
    cols_count, rows_count = (1, 1)
    for tree_level in range(levels):
        if tree_level % 2 == 0:
            merge_plan.append(("y", cols_count, rows_count))
            rows_count = rows_count * 2
        else:
            merge_plan.append(("x", cols_count, rows_count))
            cols_count = cols_count * 2
    return merge_plan


def take_rows(matrix, starts, lengths, side_name):
    return matrix[starts[side_name] : starts[side_name] + lengths[side_name]]


def take_cols(matrix, starts, lengths, side_name):
    return matrix[:, starts[side_name] : starts[side_name] + lengths[side_name]]


def take_block(matrix, starts, lengths, row_side, col_side):
    return take_cols(take_rows(matrix, starts, lengths, row_side), starts, lengths, col_side)


def product(left_part, right_part):
    return jnp.dot(left_part, right_part, precision=lax.Precision.HIGHEST)


def solve_with(factor, rhs_part):
    halfway = jax.scipy.linalg.solve_triangular(factor, rhs_part, lower=True)
    return jax.scipy.linalg.solve_triangular(factor, halfway, lower=True, trans=1)


def diagonal_rows(matrix, starts, lengths, child_index, row_side, pieces):
    blocks = []
    for other_index, col_side in pieces:
        if other_index == child_index:
            blocks.append(take_block(matrix, starts, lengths, row_side, col_side))
        else:
            blocks.append(jnp.zeros((lengths[row_side], lengths[col_side]), matrix.dtype))
    return jnp.concatenate(blocks, axis=1)


def own_rows_parts(own_map, own_flux, starts, lengths, face_sides, pieces, child_index):
    chosen = [side_name for other_index, side_name in pieces if other_index == child_index]
    inward = jnp.concatenate(
        [
            take_block(own_map, starts, lengths, side_name, face_sides[child_index])
            for side_name in chosen
        ],
        axis=0,
    )
    assembled = jnp.concatenate(
        [
            diagonal_rows(own_map, starts, lengths, child_index, side_name, pieces)
            for side_name in chosen
        ],
        axis=0,
    )
    outer_flux = jnp.concatenate(
        [take_rows(own_flux, starts, lengths, side_name) for side_name in chosen], axis=0
    )
    return (inward, assembled, outer_flux)


def merge_own_rows(
    own_map, own_flux, is_lower, direction, bit_number, cols_count, rows_count, patch_side
):
    starts, lengths = side_spans(cols_count, rows_count, patch_side)
    face_sides, pieces = merge_layout(direction)
    face_rows = jnp.where(
        is_lower,
        take_rows(own_map, starts, lengths, face_sides[0]),
        take_rows(own_map, starts, lengths, face_sides[1]),
    )
    face_flux = jnp.where(
        is_lower,
        take_rows(own_flux, starts, lengths, face_sides[0]),
        take_rows(own_flux, starts, lengths, face_sides[1]),
    )
    if direction == "y":
        partner_rows, partner_flux = from_partner((face_rows, face_flux), "gy", bit_number)
    else:
        partner_rows, partner_flux = from_partner((face_rows, face_flux), "gx", bit_number)
    rows_pair = (
        jnp.where(is_lower, face_rows, partner_rows),
        jnp.where(is_lower, partner_rows, face_rows),
    )
    flux_pair = (
        jnp.where(is_lower, face_flux, partner_flux),
        jnp.where(is_lower, partner_flux, face_flux),
    )
    interface_matrix = take_cols(rows_pair[0], starts, lengths, face_sides[0]) + take_cols(
        rows_pair[1], starts, lengths, face_sides[1]
    )
    factor = jnp.linalg.cholesky(interface_matrix)
    across = jnp.concatenate(
        [
            take_cols(rows_pair[child_index], starts, lengths, side_name)
            for child_index, side_name in pieces
        ],
        axis=1,
    )
    solved = solve_with(factor, across)
    weights = solve_with(factor, flux_pair[0] + flux_pair[1])
    lower_parts = own_rows_parts(own_map, own_flux, starts, lengths, face_sides, pieces, 0)
    upper_parts = own_rows_parts(own_map, own_flux, starts, lengths, face_sides, pieces, 1)
    inward = jnp.where(is_lower, lower_parts[0], upper_parts[0])
    assembled = jnp.where(is_lower, lower_parts[1], upper_parts[1])
    outer_flux = jnp.where(is_lower, lower_parts[2], upper_parts[2])
    merged_rows = assembled - product(inward, solved)
    merged_flux = outer_flux - product(inward, weights)
    if direction == "y":
        partner_merged, partner_merged_flux = from_partner(
            (merged_rows, merged_flux), "gy", bit_number
        )
    else:
        partner_merged, partner_merged_flux = from_partner(
            (merged_rows, merged_flux), "gx", bit_number
        )
    map_pair = (
        jnp.where(is_lower, merged_rows, partner_merged),
        jnp.where(is_lower, partner_merged, merged_rows),
    )
    merged_flux_pair = (
        jnp.where(is_lower, merged_flux, partner_merged_flux),
        jnp.where(is_lower, partner_merged_flux, merged_flux),
    )
    row_starts = [0, 0]
    map_blocks = []
    flux_blocks = []
    for child_index, side_name in pieces:
        first_row = row_starts[child_index]
        map_blocks.append(map_pair[child_index][first_row : first_row + lengths[side_name]])
        flux_blocks.append(
            merged_flux_pair[child_index][first_row : first_row + lengths[side_name]]
        )
        row_starts[child_index] = first_row + lengths[side_name]
    return (
        jnp.concatenate(map_blocks, axis=0),
        jnp.concatenate(flux_blocks, axis=0),
        solved,
        weights,
    )


def merged_length(direction, cols_count, rows_count, patch_side):
    starts, lengths = side_spans(cols_count, rows_count, patch_side)
    face_sides, pieces = merge_layout(direction)
    return sum((lengths[side_name] for child_index, side_name in pieces))


def child_values(
    group_values, face_values, direction, cols_count, rows_count, patch_side, child_index
):
    starts, lengths = side_spans(cols_count, rows_count, patch_side)
    face_sides, pieces = merge_layout(direction)
    offsets = {}
    running = 0
    for each_piece in pieces:
        offsets[each_piece] = running
        running = running + lengths[each_piece[1]]
    parts_list = []
    for side_name in side_names:
        if side_name == face_sides[child_index]:
            parts_list.append(face_values)
        else:
            first_row = offsets[child_index, side_name]
            parts_list.append(group_values[first_row : first_row + lengths[side_name]])
    return jnp.concatenate(parts_list, axis=0)


def shards(leaf_maps, leaf_fluxes):
    patch_side = leaf_maps.shape[2] // 4
    merge_plan = level_plan(LEVELS)
    own_map = leaf_maps[0, 0]
    own_flux = leaf_fluxes[0, 0]
    column_index = lax.axis_index("gx")
    row_index = lax.axis_index("gy")
    stored = []
    own_values = None
    for tree_level in range(LEVELS):
        direction, cols_count, rows_count = merge_plan[tree_level]
        bit_number = tree_level // 2
        position = row_index if direction == "y" else column_index
        is_lower = jnp.bitwise_and(jnp.right_shift(position, bit_number), 1) == 0
        if tree_level < LEVELS - 1:
            own_map, own_flux, solved, weights = merge_own_rows(
                own_map,
                own_flux,
                is_lower,
                direction,
                bit_number,
                cols_count,
                rows_count,
                patch_side,
            )
            stored.append((solved, weights, is_lower))
        else:
            starts, lengths = side_spans(cols_count, rows_count, patch_side)
            face_sides, pieces = merge_layout(direction)
            own_block = jnp.where(
                is_lower,
                take_block(own_map, starts, lengths, face_sides[0], face_sides[0]),
                take_block(own_map, starts, lengths, face_sides[1], face_sides[1]),
            )
            own_face_flux = jnp.where(
                is_lower,
                take_rows(own_flux, starts, lengths, face_sides[0]),
                take_rows(own_flux, starts, lengths, face_sides[1]),
            )
            partner_block, partner_face_flux = from_partner(
                (own_block, own_face_flux), "gx", bit_number
            )
            lower_block = jnp.where(is_lower, own_block, partner_block)
            upper_block = jnp.where(is_lower, partner_block, own_block)
            lower_face_flux = jnp.where(is_lower, own_face_flux, partner_face_flux)
            upper_face_flux = jnp.where(is_lower, partner_face_flux, own_face_flux)
            factor = jnp.linalg.cholesky(lower_block + upper_block)
            face_values = -solve_with(factor, lower_face_flux + upper_face_flux)
            group_length = merged_length(direction, cols_count, rows_count, patch_side)
            group_values = jnp.zeros((group_length, own_flux.shape[1]), own_flux.dtype)
            own_values = jnp.where(
                is_lower,
                child_values(
                    group_values, face_values, direction, cols_count, rows_count, patch_side, 0
                ),
                child_values(
                    group_values, face_values, direction, cols_count, rows_count, patch_side, 1
                ),
            )
    for tree_level in range(LEVELS - 2, -1, -1):
        direction, cols_count, rows_count = merge_plan[tree_level]
        solved, weights, is_lower = stored[tree_level]
        face_values = -(product(solved, own_values) + weights)
        own_values = jnp.where(
            is_lower,
            child_values(own_values, face_values, direction, cols_count, rows_count, patch_side, 0),
            child_values(own_values, face_values, direction, cols_count, rows_count, patch_side, 1),
        )
    return own_values[None, None]


def solution(mesh):
    in_specs = (P("gx", "gy", None, None), P("gx", "gy", None, None))
    out_specs = P("gx", "gy", None, None)
    return jax.shard_map(shards, mesh=mesh, in_specs=in_specs, out_specs=out_specs, check_vma=False)
```

profile of v0, /device:TPU:0, one launch (start us, length us, event | category | flops | bytes accessed | tf_op | source)
XLA Modules:
  0.0 652.7 jit_solution(2946917504590143284)
XLA Ops:
  7.2 11.7 %cholesky.185 = f32[128,128]{1,0:T(8,128)S(1)} custom-call(f32[128,128]{1,0:T(8,128)S(1)} %copy.8), custom_call_target="Cholesky" | custom-call | tf_op jit(solution)/shard_map/jit(cholesky)/cholesky | solution.py:145
  20.5 9.8 %custom-call.72 = f32[1,128,128]{1,2,0:T(8,128)S(1)} custom-call(f32[1,128,128]{2,1,0:T(8,128)S(1)} %copy.11), custom_call_target="InvertDiagBlocksLowerTriangular" | custom-call | tf_op jit(solution)/shard_map/jit(_solve_triangular)/triangular_solve | solution.py:80
  51.7 14.9 %collective-permute-done.2 = f32[256,768]{0,1:T(8,128)S(1)} collective-permute-done((f32[256,768]{0,1:T(8,128)S(1)}, f32[256,768]{0,1:T(8,128)S(1)}, u32[]{:S(2)}, u32[]{:S(2)}) %collective-permute-start.2) | collective-permute-done | bytes 786464 | tf_op jit(solution)/shard_map/ppermute | solution.py:19
  67.7 12.2 %cholesky.392 = f32[128,128]{1,0:T(8,128)S(1)} custom-call(f32[128,128]{1,0:T(8,128)S(1)} %cholesky.442), custom_call_target="Cholesky" | custom-call | tf_op jit(solution)/shard_map/jit(cholesky)/cholesky | solution.py:145
  80.0 9.8 %custom-call.84 = f32[1,128,128]{1,2,0:T(8,128)S(1)} custom-call(f32[1,128,128]{2,1,0:T(8,128)S(1)} %get-tuple-element.264), custom_call_target="InvertDiagBlocksLowerTriangular" | custom-call | tf_op jit(solution)/shard_map/jit(cholesky)/cholesky/custom-call.19 | solution.py:145
  92.1 11.7 %cholesky.402 = f32[128,128]{1,0:T(8,128)S(1)} custom-call(f32[128,128]{1,0:T(8,128)S(1)} %convolution_subtract_fusion.11), custom_call_target="Cholesky" | custom-call | tf_op jit(solution)/shard_map/jit(cholesky)/cholesky | solution.py:145
  110.6 19.8 %custom-call.73 = f32[2,128,128]{1,2,0:T(8,128)S(1)} custom-call(f32[2,128,128]{2,1,0:T(8,128)S(1)} %get-tuple-element.32), custom_call_target="InvertDiagBlocksLowerTriangular" | custom-call | tf_op jit(solution)/shard_map/jit(_solve_triangular)/triangular_solve | solution.py:80
  146.3 43.9 %collective-permute-done.9 = f32[256,128]{0,1:T(8,128)S(1)} collective-permute-done((f32[256,128]{0,1:T(8,128)S(1)}, f32[256,128]{0,1:T(8,128)S(1)}, u32[]{:S(2)}, u32[]{:S(2)}) %collective-permute-start.9) | collective-permute-done | bytes 131104 | tf_op jit(solution)/shard_map/ppermute | solution.py:19
  204.3 16.6 %collective-permute-done.4 = f32[256,1024]{0,1:T(8,128)S(1)} collective-permute-done((f32[256,1024]{0,1:T(8,128)S(1)}, f32[256,1024]{0,1:T(8,128)S(1)}, u32[]{:S(2)}, u32[]{:S(2)}) %collective-permute-start.4) | collective-permute-done | bytes 1048608 | tf_op jit(solution)/shard_map/ppermute | solution.py:19
  223.2 11.9 %cholesky.419 = f32[128,128]{1,0:T(8,128)S(1)} custom-call(f32[128,128]{1,0:T(8,128)S(1)} %cholesky.445), custom_call_target="Cholesky" | custom-call | tf_op jit(solution)/shard_map/jit(cholesky)/cholesky | solution.py:145
  235.3 9.8 %custom-call.85 = f32[1,128,128]{1,2,0:T(8,128)S(1)} custom-call(f32[1,128,128]{2,1,0:T(8,128)S(1)} %get-tuple-element.262), custom_call_target="InvertDiagBlocksLowerTriangular" | custom-call | tf_op jit(solution)/shard_map/jit(cholesky)/cholesky/custom-call.19 | solution.py:145
  247.4 11.7 %cholesky.429 = f32[128,128]{1,0:T(8,128)S(1)} custom-call(f32[128,128]{1,0:T(8,128)S(1)} %convolution_subtract_fusion.10), custom_call_target="Cholesky" | custom-call | tf_op jit(solution)/shard_map/jit(cholesky)/cholesky | solution.py:145
  267.2 20.1 %custom-call.74 = f32[2,128,128]{1,2,0:T(8,128)S(1)} custom-call(f32[2,128,128]{2,1,0:T(8,128)S(1)} %get-tuple-element.40), custom_call_target="InvertDiagBlocksLowerTriangular" | custom-call | tf_op jit(solution)/shard_map/jit(_solve_triangular)/triangular_solve | solution.py:80
  313.4 94.2 %collective-permute-done.11 = f32[256,128]{0,1:T(8,128)S(1)} collective-permute-done((f32[256,128]{0,1:T(8,128)S(1)}, f32[256,128]{0,1:T(8,128)S(1)}, u32[]{:S(2)}, u32[]{:S(2)}) %collective-permute-start.11) | collective-permute-done | bytes 131104 | tf_op jit(solution)/shard_map/ppermute | solution.py:19
  426.8 52.8 %collective-permute-done.13 = f32[512,128]{0,1:T(8,128)S(1)} collective-permute-done((f32[512,128]{0,1:T(8,128)S(1)}, f32[512,128]{0,1:T(8,128)S(1)}, u32[]{:S(2)}, u32[]{:S(2)}) %collective-permute-start.13) | collective-permute-done | bytes 262176 | tf_op jit(solution)/shard_map/ppermute | solution.py:19
  483.4 11.7 %cholesky.194 = f32[128,128]{1,0:T(8,128)S(1)} custom-call(f32[128,128]{1,0:T(8,128)S(1)} %cholesky.448), custom_call_target="Cholesky" | custom-call | tf_op jit(solution)/shard_map/jit(cholesky)/cholesky | solution.py:268
  495.8 10.4 %custom-call.75 = f32[1,128,128]{1,2,0:T(8,128)} custom-call(f32[1,128,128]{2,1,0:T(8,128)S(1)} %copy.26), custom_call_target="InvertDiagBlocksLowerTriangular" | custom-call | tf_op jit(solution)/shard_map/jit(cholesky)/cholesky | solution.py:268
  510.2 13.2 %cholesky.308 = f32[128,128]{1,0:T(8,128)} custom-call(f32[128,128]{1,0:T(8,128)} %cholesky.452), custom_call_target="Cholesky" | custom-call | tf_op jit(solution)/shard_map/jit(cholesky)/cholesky | solution.py:268
  528.8 11.3 %custom-call.76 = f32[1,128,128]{1,2,0:T(8,128)} custom-call(f32[1,128,128]{2,1,0:T(8,128)} %copy.29), custom_call_target="InvertDiagBlocksLowerTriangular" | custom-call | tf_op jit(solution)/shard_map/jit(cholesky)/cholesky | solution.py:268
  543.0 13.2 %cholesky.329 = f32[128,128]{1,0:T(8,128)} custom-call(f32[128,128]{1,0:T(8,128)} %cholesky.457), custom_call_target="Cholesky" | custom-call | tf_op jit(solution)/shard_map/jit(cholesky)/cholesky | solution.py:268
  559.2 11.7 %custom-call.86 = f32[1,128,128]{1,2,0:T(8,128)} custom-call(f32[1,128,128]{2,1,0:T(8,128)} %get-tuple-element.259), custom_call_target="InvertDiagBlocksLowerTriangular" | custom-call | tf_op jit(solution)/shard_map/jit(cholesky)/cholesky/custom-call.19 | solution.py:268
  572.9 12.5 %cholesky.342 = f32[128,128]{1,0:T(8,128)S(1)} custom-call(f32[128,128]{1,0:T(8,128)} %convolution_subtract_fusion.13), custom_call_target="Cholesky" | custom-call | tf_op jit(solution)/shard_map/jit(cholesky)/cholesky | solution.py:268
  591.6 9.6 %while.13 = (s32[]{:T(128)}, f32[512,512]{1,0:T(8,128)S(1)}, s32[4,2]{0,1:T(2,128)S(1)}, f32[4,128,128]{2,1,0:T(8,128)}, s32[]{:T(128)}) while((s32[]{:T(128)}, f32[512,512]{1,0:T(8,128)S(1)}, s32[4,2]{0,1:T(2,128)S(1)}, f32[4,128,128]{2,1,0:T(8,128)}, s32[]{:T(128)}) %tuple.171), condition=%wide.while_cond.4, body=%wide.while_body.4.sunk | while | flops 2 | bytes 132205 | solution.py:80
  601.2 40.3 %custom-call.77 = f32[4,128,128]{1,2,0:T(8,128)S(1)} custom-call(f32[4,128,128]{2,1,0:T(8,128)} %get-tuple-element.48), custom_call_target="InvertDiagBlocksLowerTriangular" | custom-call | tf_op jit(solution)/shard_map/jit(_solve_triangular)/triangular_solve | solution.py:80
  (547 shorter events, 177.7 us)
Async XLA Ops:
  1.6 3.5 collective-permute-start
  3.3 29.1 %copy-start.34 = (f32[128,128]{0,1:T(8,128)}, f32[128,128]{0,1:T(8,128)S(1)}, u32[]{:S(2)}) copy-start(f32[128,128]{0,1:T(8,128)S(1)} %get-tuple-element.235) | copy-start | bytes 196612
  3.3 29.1 %copy-start.26 = (f32[128,128]{0,1:T(8,128)}, f32[128,128]{0,1:T(8,128)S(1)}, u32[]{:S(2)}) copy-start(f32[128,128]{0,1:T(8,128)S(1)} %get-tuple-element.231) | copy-start | bytes 196612
  3.4 29.1 %copy-start.28 = (f32[128,128]{0,1:T(8,128)}, f32[128,128]{0,1:T(8,128)S(1)}, u32[]{:S(2)}) copy-start(f32[128,128]{0,1:T(8,128)S(1)} %get-tuple-element.234) | copy-start | bytes 196612
  3.4 29.0 %copy-start.30 = (f32[128,128]{0,1:T(8,128)}, f32[128,128]{0,1:T(8,128)S(1)}, u32[]{:S(2)}) copy-start(f32[128,128]{0,1:T(8,128)S(1)} %get-tuple-element.227) | copy-start | bytes 196612
  3.4 29.0 %copy-start.32 = (f32[128,128]{0,1:T(8,128)}, f32[128,128]{0,1:T(8,128)S(1)}, u32[]{:S(2)}) copy-start(f32[128,128]{0,1:T(8,128)S(1)} %get-tuple-element.230) | copy-start | bytes 196612
  3.4 29.0 %copy-start.21 = (f32[128,768]{0,1:T(8,128)}, f32[128,768]{0,1:T(8,128)S(1)}, u32[]{:S(2)}) copy-start(f32[128,768]{0,1:T(8,128)S(1)} %constant_dynamic-update-slice_fusion.12) | copy-start | bytes 1179652
  6.1 26.3 %copy-start.17 = (f32[128,768]{0,1:T(8,128)S(1)}, f32[128,768]{0,1:T(8,128)}, u32[]{:S(2)}) copy-start(f32[128,768]{0,1:T(8,128)} %copy-done.16) | copy-start | bytes 1179652
  34.9 3.9 collective-permute-start.1
  35.2 2.6 collective-permute-start.7
  45.8 20.9 %collective-permute-start.2 = (f32[256,768]{0,1:T(8,128)S(1)}, f32[256,768]{0,1:T(8,128)S(1)}, u32[]{:S(2)}, u32[]{:S(2)}) collective-permute-start(f32[256,768]{0,1:T(8,128)S(1)} %fusion.12), channel_id=1, source_target_pairs={{0,8},{8,0},{16,24},{24,16},{1,9},{9,1},{17,25},{25,17},{2,10},{10... | collective-permute-start | bytes 2359304 | tf_op jit(solution)/shard_map/ppermute | solution.py:19
  139.8 50.7 %collective-permute-start.3 = (f32[512,1024]{0,1:T(8,128)}, f32[512,1024]{0,1:T(8,128)}, u32[]{:S(2)}, u32[]{:S(2)}) collective-permute-start(f32[512,1024]{0,1:T(8,128)} %fusion.1), channel_id=1, source_target_pairs={{0,8},{8,0},{16,24},{24,16},{1,9},{9,1},{17,25},{25,17},{2,10},{10... | collective-permute-start | bytes 6291464 | tf_op jit(solution)/shard_map/ppermute | solution.py:19
  142.3 1.5 collective-permute-start.8
  145.1 48.2 %copy-start.64 = (f32[128,128]{0,1:T(8,128)}, f32[128,128]{0,1:T(8,128)S(1)}, u32[]{:S(2)}) copy-start(f32[128,128]{0,1:T(8,128)S(1)} %get-tuple-element.254) | copy-start | bytes 196612
  145.2 45.0 %collective-permute-start.9 = (f32[256,128]{0,1:T(8,128)S(1)}, f32[256,128]{0,1:T(8,128)S(1)}, u32[]{:S(2)}, u32[]{:S(2)}) collective-permute-start(f32[256,128]{0,1:T(8,128)S(1)} %maximum_select_fusion.13), channel_id=1, source_target_pairs={{0,8},{8,0},{16,24},{24,16},{1,9},{9,1},{17,25},{25,17},{2,10},{10... | collective-permute-start | bytes 393224 | tf_op jit(solution)/shard_map/ppermute | solution.py:19
  196.9 24.0 %collective-permute-start.4 = (f32[256,1024]{0,1:T(8,128)S(1)}, f32[256,1024]{0,1:T(8,128)S(1)}, u32[]{:S(2)}, u32[]{:S(2)}) collective-permute-start(f32[256,1024]{0,1:T(8,128)S(1)} %fusion.9), channel_id=1, source_target_pairs={{0,2},{2,0},{1,3},{3,1},{4,6},{6,4},{5,7},{7,5},{8,10},{10,8},{9,1... | collective-permute-start | bytes 3145736 | tf_op jit(solution)/shard_map/ppermute | solution.py:19
  302.7 115.9 %collective-permute-start.5 = (f32[768,1536]{0,1:T(8,128)}, f32[768,1536]{0,1:T(8,128)}, u32[]{:S(2)}, u32[]{:S(2)}) collective-permute-start(f32[768,1536]{0,1:T(8,128)} %fusion), channel_id=1, source_target_pairs={{0,2},{2,0},{1,3},{3,1},{4,6},{6,4},{5,7},{7,5},{8,10},{10,8},{9,1... | collective-permute-start | bytes 14155784 | tf_op jit(solution)/shard_map/ppermute | solution.py:19
  305.9 6.4 collective-permute-start.10
  312.5 95.1 %collective-permute-start.11 = (f32[256,128]{0,1:T(8,128)S(1)}, f32[256,128]{0,1:T(8,128)S(1)}, u32[]{:S(2)}, u32[]{:S(2)}) collective-permute-start(f32[256,128]{0,1:T(8,128)S(1)} %maximum_select_fusion.14), channel_id=1, source_target_pairs={{0,2},{2,0},{1,3},{3,1},{4,6},{6,4},{5,7},{7,5},{8,10},{10,8},{9,1... | collective-permute-start | bytes 393224 | tf_op jit(solution)/shard_map/ppermute | solution.py:19
  410.4 8.3 %collective-permute-start.12 = (f32[768,128]{0,1:T(8,128)S(1)}, f32[768,128]{0,1:T(8,128)S(1)}, u32[]{:S(2)}, u32[]{:S(2)}) collective-permute-start(f32[768,128]{0,1:T(8,128)S(1)} %fusion.19), channel_id=1, source_target_pairs={{0,2},{2,0},{1,3},{3,1},{4,6},{6,4},{5,7},{7,5},{8,10},{10,8},{9,1... | collective-permute-start | bytes 1179656 | tf_op jit(solution)/shard_map/ppermute | solution.py:19
  423.7 56.7 %collective-permute-start.6 = (f32[512,512]{0,1:T(8,128)S(1)}, f32[512,512]{0,1:T(8,128)}, u32[]{:S(2)}, u32[]{:S(2)}) collective-permute-start(f32[512,512]{0,1:T(8,128)S(1)} %fusion.10), channel_id=1, source_target_pairs={{0,16},{16,0},{8,24},{24,8},{1,17},{17,1},{9,25},{25,9},{2,18},{18... | collective-permute-start | bytes 3145736 | tf_op jit(solution)/shard_map/ppermute | solution.py:19
  425.8 53.8 %collective-permute-start.13 = (f32[512,128]{0,1:T(8,128)S(1)}, f32[512,128]{0,1:T(8,128)S(1)}, u32[]{:S(2)}, u32[]{:S(2)}) collective-permute-start(f32[512,128]{0,1:T(8,128)S(1)} %maximum_select_fusion.9), channel_id=1, source_target_pairs={{0,16},{16,0},{8,24},{24,8},{1,17},{17,1},{9,25},{25,9},{2,18},{18... | collective-permute-start | bytes 786440 | tf_op jit(solution)/shard_map/ppermute | solution.py:19
  483.4 23.8 %copy-start.3 = (f32[512,512]{1,0:T(8,128)S(1)}, f32[512,512]{1,0:T(8,128)}, u32[]{:S(2)}) copy-start(f32[512,512]{1,0:T(8,128)} %copy-done.2) | copy-start | bytes 3145732
  591.6 52.9 %copy-start.6 = (f32[512,128]{0,1:T(8,128)S(1)}, f32[512,128]{0,1:T(8,128)}, u32[]{:S(2)}) copy-start(f32[512,128]{0,1:T(8,128)} %select_add_fusion.1) | copy-start | bytes 786436
  (93 other events, 352.5 us)
where the time goes:
time: 663 us; the launch traced here: 653 us
  other arithmetic  281 us (42%)
  waiting for transfers between devices  236 us (36%)
  local copies, waits for them, and re-layouts  60.6 us (9%)
  matrix products  51.8 us (8%)
  starting transfers between devices  15.5 us (2%)
  between operations  8.02 us (1%)
    ppermute x14, waiting for transfers between devices, from_partner(): return lax.ppermute(block, axis, route)  236 us
    another operation x10, other arithmetic, solve_with(): jax.scipy.linalg.solve_triangular(factor, halfway, lower=True, trans=1)  90.9 us
    another operation x16, other arithmetic, shards(): factor = jnp.linalg.cholesky(lower_block + upper_block)  90.6 us
    another operation x17, other arithmetic, merge_own_rows(): factor = jnp.linalg.cholesky(interface_matrix)  82.4 us
    unnamed x286, local copies, waits for them, and re-layouts  23.4 us
    dot_general x9, matrix products, product(): return jnp.dot(left_part, right_part, precision=lax.Precision.HIGHEST)  19.2 us
    another operation x33, local copies, waits for them, and re-layouts  17.9 us
    ppermute x14, starting transfers between devices, from_partner(): return lax.ppermute(block, axis, route)  15.5 us
  transfers between devices with their start and end apart: 14, of which 9 were waited for; matrix products, arithmetic and copies ran while one was open for 3% of the time, Pallas kernels for 0%

commit v1 on v0

v1 whole, which is shorter than its diff:
```python
import jax
import jax.numpy as jnp
from jax import lax
from jax.experimental import pallas as pl
from jax.experimental.pallas import tpu as pltpu
from jax.sharding import PartitionSpec as P

F32 = jnp.float32
HIGHEST = lax.Precision.HIGHEST
ROWS_DIM = (((0,), (0,)), ((), ()))
PANEL = 16


def dot(left, right):
    return jnp.dot(left, right, precision=HIGHEST, preferred_element_type=F32)


def tdot(left, right):
    return lax.dot_general(
        left, right, ROWS_DIM, precision=HIGHEST, preferred_element_type=F32
    )


def three_parts(x):
    first = x.astype(jnp.bfloat16)
    rest = x - first.astype(F32)
    second = rest.astype(jnp.bfloat16)
    third = (rest - second.astype(F32)).astype(jnp.bfloat16)
    return first, second, third


def tdot_thin(left, right):
    a, b, c = three_parts(left)
    d, e, f = three_parts(right)
    return lax.dot_general(
        jnp.concatenate([a, a, b, b, a, c], axis=0),
        jnp.concatenate([d, e, d, e, f, d], axis=0),
        ROWS_DIM,
        preferred_element_type=F32,
    )


def panel_solve(rows, rhs, first):
    width, lanes = rows.shape
    sub = lax.broadcasted_iota(jnp.int32, (width, lanes), 0)
    cols = [
        jnp.broadcast_to(rows[:, first + j : first + j + 1], (width, lanes))
        for j in range(width)
    ]
    for j in range(0, width, 2):
        c0, c1 = cols[j], cols[j + 1]
        aa, bb, dd = c0[j : j + 1], c1[j : j + 1], c1[j + 1 : j + 2]
        scale = 1.0 / (aa * dd - bb * bb)
        aa, bb, dd = aa * scale, bb * scale, dd * scale

        def step(x):
            x0, x1 = x[j : j + 1], x[j + 1 : j + 2]
            r0 = dd * x0 - bb * x1
            r1 = aa * x1 - bb * x0
            y = x - c0 * r0 - c1 * r1
            return jnp.where(sub == j, r0, jnp.where(sub == j + 1, r1, y))

        rhs = step(rhs)
        for m in range(j + 2, width):
            cols[m] = step(cols[m])
    return rhs


def spd_inverse(a):
    size = a.shape[0]
    row = lax.broadcasted_iota(jnp.int32, (PANEL, size), 0)
    col = lax.broadcasted_iota(jnp.int32, (PANEL, size), 1)
    for first in range(0, size, PANEL):
        rows = a[first : first + PANEL]
        v = rows - jnp.where(col == row + first, 1.0, 0.0)
        a = a - tdot_thin(v, panel_solve(rows, v, first))
    row = lax.broadcasted_iota(jnp.int32, (size, size), 0)
    col = lax.broadcasted_iota(jnp.int32, (size, size), 1)
    return jnp.where(row == col, 2.0, 0.0) - a


def block_solve(g, face, p, schur=None):
    for k in range(0, face, p):
        head = g[k : k + p, k + p :]
        t = dot(spd_inverse(g[k : k + p, k : k + p]), head)
        if k + p < face:
            g[k + p : face, k + p :] -= tdot(head[:, : face - k - p], t)
        if schur is not None:
            outer = head[:, face - k - p : face - k - p + schur.shape[0]]
            schur[...] -= tdot(outer, t[:, face - k - p :])
        g[k : k + p, k + p :] = t
    for k in range(face - 2 * p, -1, -p):
        g[k : k + p, face:] -= dot(g[k : k + p, k + p : face], g[k + p : face, face:])


def leaf_merge(own_map, own_flux, other_map, other_flux, n_ref, y_ref, send_ref, g):
    p = own_map.shape[0] // 4
    gx, gy = lax.axis_index("gx"), lax.axis_index("gy")
    lower = gy % 2 == 0
    low_group = (gy // 2) % 2 == 0
    f1 = pl.multiple_of(p * (1 - gx % 2), p)
    out = pl.multiple_of(p * (gx % 2), p)
    bottom, top = 2 * p, 3 * p

    def lo(r, c):
        at = (pl.ds(r, p), pl.ds(c, p))
        return jnp.where(lower, own_map[at], other_map[at])

    def up(r, c):
        at = (pl.ds(r, p), pl.ds(c, p))
        return jnp.where(lower, other_map[at], own_map[at])

    def lo_h(r):
        return jnp.where(lower, own_flux[pl.ds(r, p), :], other_flux[pl.ds(r, p), :])

    def up_h(r):
        return jnp.where(lower, other_flux[pl.ds(r, p), :], own_flux[pl.ds(r, p), :])

    g[:, 0:p] = lo(top, top) + up(bottom, bottom)
    g[:, p : 2 * p] = lo(top, f1)
    g[:, 2 * p : 3 * p] = up(bottom, f1)
    g[:, 3 * p : 4 * p] = jnp.where(low_group, up(bottom, top), lo(top, bottom))
    g[:, 4 * p : 5 * p] = lo(top, out)
    g[:, 5 * p : 6 * p] = up(bottom, out)
    g[:, 6 * p :] = lo_h(top) + up_h(bottom)
    none = jnp.zeros((p, p), F32)
    from_lo = jnp.where(low_group, 0.0, 1.0)
    from_up = 1.0 - from_lo
    blocks = [
        [lo(f1, f1), none, lo(f1, bottom) * from_lo, lo(f1, out), none, lo_h(f1)],
        [none, up(f1, f1), up(f1, top) * from_up, none, up(f1, out), up_h(f1)],
        [
            lo(bottom, f1) * from_lo,
            up(top, f1) * from_up,
            jnp.where(low_group, up(top, top), lo(bottom, bottom)),
            lo(bottom, out) * from_lo,
            up(top, out) * from_up,
            jnp.where(low_group, up_h(top), lo_h(bottom)),
        ],
        [lo(out, f1), none, lo(out, bottom) * from_lo, lo(out, out), none, lo_h(out)],
        [none, up(out, f1), up(out, top) * from_up, none, up(out, out), up_h(out)],
    ]
    for i, line in enumerate(blocks):
        for j, block in enumerate(line):
            n_ref[i * p : (i + 1) * p, j * p : j * p + block.shape[1]] = block
    block_solve(g, p, p, n_ref)
    y_ref[...] = g[:, p:]
    half = 3 * p // 2
    mine = pl.ds(pl.multiple_of((gy % 2) * half, half), half)
    send_ref[:, : 3 * p] = n_ref[mine, : 3 * p]
    send_ref[:, 3 * p :] = n_ref[mine, 5 * p :]


def column_merge(n0, got, swapped, n_ref, y_ref, send2_ref, send3_ref, g, q):
    p = n0.shape[0] // 5
    core = lax.axis_index("gy") % 2
    half = 3 * p // 2
    q[pl.ds(pl.multiple_of(core * half, half), half), :] = got[...]
    q[pl.ds(pl.multiple_of((1 - core) * half, half), half), :] = swapped[...]
    f, o, e = 2 * p, 3 * p, 5 * p
    g[:, 0:f] = n0[0:f, 0:f] + q[0:f, 0:f]
    g[:, f : f + p] = n0[0:f, f:o]
    g[:, f + p : f + 2 * p] = q[0:f, f:o]
    g[:, f + 2 * p : f + 4 * p] = n0[0:f, o:e]
    g[:, f + 4 * p :] = n0[0:f, e:] + q[0:f, o:]
    n_ref[...] = jnp.zeros_like(n_ref)
    n_ref[0:p, 0:p] = n0[f:o, f:o]
    n_ref[0:p, 2 * p :] = n0[f:o, o:]
    n_ref[p : 2 * p, p : 2 * p] = q[f:o, f:o]
    n_ref[p : 2 * p, 4 * p :] = q[f:o, o:]
    n_ref[2 * p :, 0:p] = n0[o:, f:o]
    n_ref[2 * p :, 2 * p :] = n0[o:, o:]
    block_solve(g, f, p, n_ref)
    y_ref[...] = g[:, f:]
    send2_ref[...] = n_ref[pl.ds(pl.multiple_of(core * p, p), p), :]
    send3_ref[...] = n_ref[pl.ds(pl.multiple_of((2 + core) * p, p), p), 2 * p :]


def row_merge(n1, got2, got3, swap2, swap3, n_ref, y_ref, send_ref, g, q2, q3):
    p = n1.shape[0] // 4
    core = lax.axis_index("gy") % 2
    here = pl.ds(pl.multiple_of(core * p, p), p)
    there = pl.ds(pl.multiple_of((1 - core) * p, p), p)
    q2[here, :] = got2[...]
    q2[there, :] = swap2[...]
    q3[here, :] = got3[...]
    q3[there, :] = swap3[...]
    f = 2 * p
    g[:, 0:f] = n1[0:f, 0:f] + q2[:, 0:f]
    g[:, f : 2 * f] = n1[0:f, f : 2 * f]
    g[:, 2 * f : 3 * f] = q2[:, f : 2 * f]
    g[:, 3 * f :] = n1[0:f, 2 * f :] + q2[:, 2 * f :]
    n_ref[...] = jnp.zeros_like(n_ref)
    n_ref[0:f, 0:f] = n1[f:, f : 2 * f]
    n_ref[0:f, 2 * f :] = n1[f:, 2 * f :]
    n_ref[f:, f:] = q3[...]
    block_solve(g, f, p, n_ref)
    y_ref[...] = g[:, f:]
    send_ref[...] = n_ref[pl.ds(pl.multiple_of(core * f, f), f), :]


def top_solve(n2, got, swapped, y2, y1, u_ref, send_ref, g):
    p = n2.shape[0] // 4
    core = lax.axis_index("gy") % 2
    f = 2 * p
    here = pl.ds(pl.multiple_of(core * f, f), f)
    there = pl.ds(pl.multiple_of((1 - core) * f, f), f)
    g[here, :] = n2[here, :] + got[...]
    g[there, :] = n2[there, :] + swapped[...]
    block_solve(g, 4 * p, p)
    u3 = -g[:, 4 * p :]
    u2 = -(dot(y2[:, : 4 * p], u3) + y2[:, 4 * p :])
    u_ref[3 * p :, :] = u3[0:f]
    group = jnp.concatenate([u2, u3[0:f]], axis=0)
    u1 = -(dot(y1[:, : 4 * p], group) + y1[:, 4 * p :])
    u_ref[0:f, :] = u1
    u_ref[f : 3 * p, :] = u2[0:p]
    send_ref[0:f, :] = u1
    send_ref[f:, :] = u2[p:]


def leaf_values(own, got, y0, out_ref, u):
    p = own.shape[0] // 5
    gx, gy = lax.axis_index("gx"), lax.axis_index("gy")
    inner = (gx + 1) // 2 % 2 == 1
    lower = gy % 2 == 0
    low_group = (gy // 2) % 2 == 0
    u[0 : 3 * p, :] = jnp.where(inner, own[0 : 3 * p, :], got[...])
    u[3 * p :, :] = jnp.where(inner, own[3 * p :, :], 0.0)
    face = -(dot(y0[:, : 5 * p], u[...]) + y0[:, 5 * p :])
    spot = gy % 2
    near = u[pl.ds(pl.multiple_of(spot * p, p), p), :]
    far = u[pl.ds(pl.multiple_of((3 + spot) * p, p), p), :]
    cross = u[2 * p : 3 * p, :]
    f1_left = gx % 2 == 1
    out_ref[0:p, :] = jnp.where(f1_left, near, far)
    out_ref[p : 2 * p, :] = jnp.where(f1_left, far, near)
    out_ref[2 * p : 3 * p, :] = jnp.where(lower, jnp.where(low_group, 0.0, cross), face)
    out_ref[3 * p :, :] = jnp.where(lower, face, jnp.where(low_group, cross, 0.0))


def local(kernel, name, outs, scratch, *args):
    specs = [pl.BlockSpec(memory_space=pltpu.VMEM)]
    return pl.pallas_call(
        kernel,
        name=name,
        out_shape=[jax.ShapeDtypeStruct(shape, F32) for shape in outs],
        in_specs=specs * len(args),
        out_specs=specs * len(outs),
        scratch_shapes=[pltpu.VMEM(shape, F32) for shape in scratch],
        compiler_params=pltpu.CompilerParams(vmem_limit_bytes=48 << 20),
    )(*args)


def shards(leaf_maps, leaf_fluxes):
    p = leaf_maps.shape[2] // 4
    s = leaf_fluxes.shape[3]
    own_map, own_flux = leaf_maps[0, 0], leaf_fluxes[0, 0]
    columns, rows = lax.axis_size("gx"), lax.axis_size("gy")
    cores = [(i, i ^ 1) for i in range(rows)]
    groups = [(i, i ^ 2) for i in range(rows)]
    inner = [i for i in range(columns) if (i + 1) // 2 % 2 == 1]
    inward = [(i ^ 1, i) for i in inner]
    across = [(i, i ^ 3) for i in inner]
    outward = [(i, i ^ 1) for i in inner]

    def swap(x):
        return lax.ppermute(x, "gy", cores)

    other_map, other_flux = swap((own_map, own_flux))
    n0, y0, send = local(
        leaf_merge,
        "leaf_merge",
        [(5 * p, 5 * p + s), (p, 5 * p + s), (3 * p // 2, 3 * p + s)],
        [(p, 6 * p + s)],
        own_map,
        own_flux,
        other_map,
        other_flux,
    )
    got = lax.ppermute(send, "gx", inward)
    n1, y1, send2, send3 = local(
        column_merge,
        "column_merge",
        [(4 * p, 4 * p + s), (2 * p, 4 * p + s), (p, 4 * p + s), (p, 2 * p + s)],
        [(2 * p, 6 * p + s), (3 * p, 3 * p + s)],
        n0,
        got,
        swap(got),
    )
    got2, got3 = lax.ppermute((send2, send3), "gy", groups)
    swap2, swap3 = swap((got2, got3))
    n2, y2, send = local(
        row_merge,
        "row_merge",
        [(4 * p, 4 * p + s), (2 * p, 4 * p + s), (2 * p, 4 * p + s)],
        [(2 * p, 6 * p + s), (2 * p, 4 * p + s), (2 * p, 2 * p + s)],
        n1,
        got2,
        got3,
        swap2,
        swap3,
    )
    got = lax.ppermute(send, "gx", across)
    u, send = local(
        top_solve,
        "top_solve",
        [(5 * p, s), (3 * p, s)],
        [(4 * p, 4 * p + s)],
        n2,
        got,
        swap(got),
        y2,
        y1,
    )
    got = lax.ppermute(send, "gx", outward)
    (values,) = local(leaf_values, "leaf_values", [(4 * p, s)], [(5 * p, s)], u, got, y0)
    return values[None, None]


def solution(mesh):
    spec = P("gx", "gy", None, None)
    return jax.shard_map(
        shards, mesh=mesh, in_specs=(spec, spec), out_specs=spec, check_vma=False
    )
```

time: 663 us -> 114 us (0.17); the launches traced: 653 us -> 113 us
  other arithmetic: 281 us -> 0 us
  waiting for transfers between devices: 236 us -> 53.9 us
  local copies, waits for them, and re-layouts: 60.6 us -> 2.17 us
  matrix products: 51.8 us -> 0 us
  Pallas kernels: 0 us -> 47.3 us
  between operations: 8.02 us -> 0.08 us
    another operation x43 -> x0, other arithmetic: 264 us -> none  [the longest x10 90.9 us: solve_with(): jax.scipy.linalg.solve_triangular(factor, halfway, lower=True, trans=1)]
    ppermute x14 -> x11, waiting for transfers between devices: 236 us -> 53.9 us  [the longest x1 25.6 us: shards(): got = lax.ppermute(send, 'gx', outward)]
    pallas_call x0 -> x5, Pallas kernels: none -> 47.3 us  [local(): pl.pallas_call(kernel, name=name, out_shape=[jax.ShapeDtypeStruct(shape,...]
    another operation x52 -> x0, matrix products: 32.6 us -> none  [the longest x21 14.8 us: solve_with(): halfway = jax.scipy.linalg.solve_triangular(factor, rhs_part, lower=True)]
    another operation x59 -> x0, local copies, waits for them, and re-layouts: 26.6 us -> none
    unnamed x286 -> x4, local copies, waits for them, and re-layouts: 23.4 us -> 2.17 us
    dot_general x9 -> x0, matrix products: 19.2 us -> none  [product(): return jnp.dot(left_part, right_part, precision=lax.Precision.HIGHEST)]
    select_n x21 -> x0, other arithmetic: 11.3 us -> none  [the longest x3 8.6 us: merge_own_rows(): jnp.where(is_lower, merged_rows, partner_merged)]
  transfers between devices with their start and end apart: 14 -> 11, of which waited for: 9 -> 8; matrix products, arithmetic and copies ran while one was open for 3% -> 0% of each run, Pallas kernels for 0% -> 0%
where the time goes in v1:
time: 114 us; the launch traced here: 113 us
  waiting for transfers between devices  53.9 us (47%)
  Pallas kernels  47.3 us (41%)
  starting transfers between devices  9.87 us (9%)
  local copies, waits for them, and re-layouts  2.17 us (2%)
    pallas_call x5, Pallas kernels, local(): pl.pallas_call(kernel, name=name, out_shape=[jax.ShapeDtypeStruct(shape,...  47.3 us
    ppermute x1, waiting for transfers between devices, shards(): got = lax.ppermute(send, 'gx', outward)  25.6 us
    ppermute x2, waiting for transfers between devices, shards(): got2, got3 = lax.ppermute((send2, send3), 'gy', groups)  11.9 us
    ppermute x1, waiting for transfers between devices, shards(): got = lax.ppermute(send, 'gx', inward)  8.45 us
    ppermute x6, waiting for transfers between devices, swap(): return lax.ppermute(x, 'gy', cores)  7.93 us
    ppermute x1, starting transfers between devices, shards(): got = lax.ppermute(send, 'gx', inward)  5.05 us
  transfers between devices with their start and end apart: 11, of which 8 were waited for; matrix products, arithmetic and copies ran while one was open for 0% of the time, Pallas kernels for 0%

profile of v1, /device:TPU:0, one launch (start us, length us, event | category | flops | bytes accessed | tf_op | source)
XLA Modules:
  0.0 113.3 jit_solution(17325160491497069475)
XLA Ops:
  0.0 0.5 collective-permute-start
  0.5 0.1 collective-permute-start.1
  0.5 2.8 %collective-permute-done.1.other_flux = f32[512,128]{1,0:T(8,128)S(1)} collective-permute-done((f32[512,128]{1,0:T(8,128)}, f32[512,128]{1,0:T(8,128)S(1)}, u32[]{:S(2)}, u32[]{:S(2)}) %collective-permute-start.1) | collective-permute-done | bytes 262176 | tf_op jit(solution)/shard_map/ppermute | solution.py:268
  3.3 1.2 %copy-done = f32[1,1,512,512]{3,2,1,0:T(8,128)S(1)} copy-done((f32[1,1,512,512]{3,2,1,0:T(8,128)S(1)}, f32[1,1,512,512]{3,2,1,0:T(8,128)}, u32[]{:S(2)}) %copy-start) | copy-done | bytes 1048600
  4.6 0.9 copy-done.1
  5.5 5.7 %leaf_merge.1 = (f32[640,768]{1,0:T(8,128)S(1)}, f32[128,768]{1,0:T(8,128)S(1)}, f32[192,512]{1,0:T(8,128)S(1)}) custom-call(f32[512,512]{1,0:T(8,128)S(1)} %bitcast.4, f32[512,128]{1,0:T(8,128)S(1)} %bitcast.6, f32[512,512]{1,0:T(8,128)S(1)} %collective-permute-done.other_map, f32[512,128]{1,0:T(8,128)S(1)} %collective-permute-done.1.other_flux), custom_call_target="tpu_custom_call" | custom-call | tf_op jit(solution)/shard_map/leaf_merge/pallas_call | solution.py:244
  11.2 5.1 %collective-permute-start.2 = (f32[192,512]{1,0:T(8,128)S(1)}, f32[192,512]{1,0:T(8,128)S(1)}, u32[]{:S(2)}, u32[]{:S(2)}) collective-permute-start(f32[192,512]{1,0:T(8,128)S(1)} %get-tuple-element.18), channel_id=1, source_target_pairs={{0,8},{24,16},{1,9},{25,17},{2,10},{26,18},{3,11},{27,19},{4,12},{... | collective-permute-start | bytes 1179656 | tf_op jit(solution)/shard_map/ppermute | solution.py:281
  16.3 8.5 %collective-permute-done.2.got = f32[192,512]{1,0:T(8,128)S(1)} collective-permute-done((f32[192,512]{1,0:T(8,128)S(1)}, f32[192,512]{1,0:T(8,128)S(1)}, u32[]{:S(2)}, u32[]{:S(2)}) %collective-permute-start.2) | collective-permute-done | bytes 393248 | tf_op jit(solution)/shard_map/ppermute | solution.py:281
  24.7 1.7 %collective-permute-done.3.swapped = f32[192,512]{1,0:T(8,128)S(1)} collective-permute-done((f32[192,512]{1,0:T(8,128)S(1)}, f32[192,512]{1,0:T(8,128)S(1)}, u32[]{:S(2)}, u32[]{:S(2)}) %collective-permute-start.3) | collective-permute-done | bytes 393248 | tf_op jit(solution)/shard_map/ppermute | solution.py:268
  26.5 10.3 %column_merge.1 = (f32[512,640]{1,0:T(8,128)S(1)}, f32[256,640]{1,0:T(8,128)S(1)}, f32[128,640]{1,0:T(8,128)S(1)}, f32[128,384]{1,0:T(8,128)S(1)}) custom-call(f32[640,768]{1,0:T(8,128)S(1)} %get-tuple-element.17.n0, f32[192,512]{1,0:T(8,128)S(1)} %collective-permute-done.2.got, f32[192,512]{1,0:T(8,128)S(1)} %collective-permute-done.3.swapped), custom_call_target="tpu_custom_call" | custom-call | tf_op jit(solution)/shard_map/column_merge/pallas_call | solution.py:244
  36.8 1.6 %collective-permute-start.4 = (f32[128,640]{1,0:T(8,128)S(1)}, f32[128,640]{1,0:T(8,128)S(1)}, u32[]{:S(2)}, u32[]{:S(2)}) collective-permute-start(f32[128,640]{1,0:T(8,128)S(1)} %get-tuple-element.20), channel_id=1, source_target_pairs={{0,2},{1,3},{2,0},{3,1},{4,6},{5,7},{6,4},{7,5},{8,10},{9,11},{10,... | collective-permute-start | bytes 983048 | tf_op jit(solution)/shard_map/ppermute | solution.py:291
  38.3 0.5 collective-permute-start.5
  38.9 8.5 %collective-permute-done.4.got2 = f32[128,640]{1,0:T(8,128)S(1)} collective-permute-done((f32[128,640]{1,0:T(8,128)S(1)}, f32[128,640]{1,0:T(8,128)S(1)}, u32[]{:S(2)}, u32[]{:S(2)}) %collective-permute-start.4) | collective-permute-done | bytes 327712 | tf_op jit(solution)/shard_map/ppermute | solution.py:291
  47.4 3.4 %collective-permute-done.5.got3 = f32[128,384]{1,0:T(8,128)S(1)} collective-permute-done((f32[128,384]{1,0:T(8,128)S(1)}, f32[128,384]{1,0:T(8,128)S(1)}, u32[]{:S(2)}, u32[]{:S(2)}) %collective-permute-start.5) | collective-permute-done | bytes 196640 | tf_op jit(solution)/shard_map/ppermute | solution.py:291
  50.8 0.0 collective-permute-start.7
  50.8 1.4 %collective-permute-done.7.swap3 = f32[128,384]{1,0:T(8,128)S(1)} collective-permute-done((f32[128,384]{1,0:T(8,128)S(1)}, f32[128,384]{1,0:T(8,128)S(1)}, u32[]{:S(2)}, u32[]{:S(2)}) %collective-permute-start.7) | collective-permute-done | bytes 196640 | tf_op jit(solution)/shard_map/ppermute | solution.py:268
  52.3 10.6 %row_merge.1 = (f32[512,640]{1,0:T(8,128)S(1)}, f32[256,640]{1,0:T(8,128)S(1)}, f32[256,640]{1,0:T(8,128)S(1)}) custom-call(f32[512,640]{1,0:T(8,128)S(1)} %get-tuple-element.19.n1, f32[128,640]{1,0:T(8,128)S(1)} %collective-permute-done.4.got2, f32[128,384]{1,0:T(8,128)S(1)} %collective-permute-done.5.got3, f32[128,640]{1,0:T(8,128)S(1)} %collective-permute-done.6.swap2, ...), custom_call_target="tpu_custom_call" | custom-call | tf_op jit(solution)/shard_map/row_merge/pallas_call | solution.py:244
  62.9 0.7 collective-permute-start.8
  63.6 0.2 collective-permute-start.9
  63.8 2.0 %collective-permute-done.9.swapped = f32[256,640]{1,0:T(8,128)S(1)} collective-permute-done((f32[256,640]{1,0:T(8,128)S(1)}, f32[256,640]{1,0:T(8,128)S(1)}, u32[]{:S(2)}, u32[]{:S(2)}) %collective-permute-start.9) | collective-permute-done | bytes 655392 | tf_op jit(solution)/shard_map/ppermute | solution.py:268
  65.8 19.5 %top_solve.1 = (f32[640,128]{1,0:T(8,128)S(1)}, f32[384,128]{1,0:T(8,128)S(1)}) custom-call(f32[512,640]{1,0:T(8,128)S(1)} %get-tuple-element.22.n2, f32[256,640]{1,0:T(8,128)S(1)} %collective-permute-done.8.got, f32[256,640]{1,0:T(8,128)S(1)} %collective-permute-done.9.swapped, f32[256,640]{1,0:T(8,128)S(1)} %get-tuple-element.24.y2, ...), custom_call_target="tpu_custom_call" | custom-call | tf_op jit(solution)/shard_map/top_solve/pallas_call | solution.py:244
  85.2 1.3 %collective-permute-start.10 = (f32[384,128]{1,0:T(8,128)S(1)}, f32[384,128]{1,0:T(8,128)S(1)}, u32[]{:S(2)}, u32[]{:S(2)}) collective-permute-start(f32[384,128]{1,0:T(8,128)S(1)} %get-tuple-element.27), channel_id=1, source_target_pairs={{8,0},{16,24},{9,1},{17,25},{10,2},{18,26},{11,3},{19,27},{12,4},{... | collective-permute-start | bytes 589832 | tf_op jit(solution)/shard_map/ppermute | solution.py:316
  86.5 25.6 %collective-permute-done.10.got = f32[384,128]{1,0:T(8,128)S(1)} collective-permute-done((f32[384,128]{1,0:T(8,128)S(1)}, f32[384,128]{1,0:T(8,128)S(1)}, u32[]{:S(2)}, u32[]{:S(2)}) %collective-permute-start.10) | collective-permute-done | bytes 196640 | tf_op jit(solution)/shard_map/ppermute | solution.py:316
  112.1 1.2 %leaf_values.1 = f32[512,128]{1,0:T(8,128)} custom-call(f32[640,128]{1,0:T(8,128)S(1)} %get-tuple-element.26.own, f32[384,128]{1,0:T(8,128)S(1)} %collective-permute-done.10.got, f32[128,768]{1,0:T(8,128)S(1)} %get-tuple-element.28.y0), custom_call_target="tpu_custom_call" | custom-call | tf_op jit(solution)/shard_map/leaf_values/pallas_call | solution.py:244
  (7 shorter events, 0.0 us)
Async XLA Ops:
  0.0 3.3 %collective-permute-start = (f32[512,512]{1,0:T(8,128)}, f32[512,512]{1,0:T(8,128)S(1)}, u32[]{:S(2)}, u32[]{:S(2)}) collective-permute-start(f32[512,512]{1,0:T(8,128)} %bitcast.3), channel_id=1, source_target_pairs={{0,1},{1,0},{2,3},{3,2},{4,5},{5,4},{6,7},{7,6},{8,9},{9,8},{10,11... | collective-permute-start | bytes 3145736 | tf_op jit(solution)/shard_map/ppermute | solution.py:268
  0.5 2.9 %collective-permute-start.1 = (f32[512,128]{1,0:T(8,128)}, f32[512,128]{1,0:T(8,128)S(1)}, u32[]{:S(2)}, u32[]{:S(2)}) collective-permute-start(f32[512,128]{1,0:T(8,128)} %bitcast.5), channel_id=1, source_target_pairs={{0,1},{1,0},{2,3},{3,2},{4,5},{5,4},{6,7},{7,6},{8,9},{9,8},{10,11... | collective-permute-start | bytes 786440 | tf_op jit(solution)/shard_map/ppermute | solution.py:268
  3.3 1.2 %copy-start = (f32[1,1,512,512]{3,2,1,0:T(8,128)S(1)}, f32[1,1,512,512]{3,2,1,0:T(8,128)}, u32[]{:S(2)}) copy-start(f32[1,1,512,512]{3,2,1,0:T(8,128)} %param.2) | copy-start | bytes 3145732
  4.6 0.9 copy-start.1
  11.2 13.5 %collective-permute-start.2 = (f32[192,512]{1,0:T(8,128)S(1)}, f32[192,512]{1,0:T(8,128)S(1)}, u32[]{:S(2)}, u32[]{:S(2)}) collective-permute-start(f32[192,512]{1,0:T(8,128)S(1)} %get-tuple-element.18), channel_id=1, source_target_pairs={{0,8},{24,16},{1,9},{25,17},{2,10},{26,18},{3,11},{27,19},{4,12},{... | collective-permute-start | bytes 1179656 | tf_op jit(solution)/shard_map/ppermute | solution.py:281
  24.7 1.7 %collective-permute-start.3 = (f32[192,512]{1,0:T(8,128)S(1)}, f32[192,512]{1,0:T(8,128)S(1)}, u32[]{:S(2)}, u32[]{:S(2)}) collective-permute-start(f32[192,512]{1,0:T(8,128)S(1)} %collective-permute-done.2.got), channel_id=1, source_target_pairs={{0,1},{1,0},{2,3},{3,2},{4,5},{5,4},{6,7},{7,6},{8,9},{9,8},{10,11... | collective-permute-start | bytes 1179656 | tf_op jit(solution)/shard_map/ppermute | solution.py:268
  36.8 10.6 %collective-permute-start.4 = (f32[128,640]{1,0:T(8,128)S(1)}, f32[128,640]{1,0:T(8,128)S(1)}, u32[]{:S(2)}, u32[]{:S(2)}) collective-permute-start(f32[128,640]{1,0:T(8,128)S(1)} %get-tuple-element.20), channel_id=1, source_target_pairs={{0,2},{1,3},{2,0},{3,1},{4,6},{5,7},{6,4},{7,5},{8,10},{9,11},{10,... | collective-permute-start | bytes 983048 | tf_op jit(solution)/shard_map/ppermute | solution.py:291
  38.3 12.5 %collective-permute-start.5 = (f32[128,384]{1,0:T(8,128)S(1)}, f32[128,384]{1,0:T(8,128)S(1)}, u32[]{:S(2)}, u32[]{:S(2)}) collective-permute-start(f32[128,384]{1,0:T(8,128)S(1)} %get-tuple-element.21), channel_id=1, source_target_pairs={{0,2},{1,3},{2,0},{3,1},{4,6},{5,7},{6,4},{7,5},{8,10},{9,11},{10,... | collective-permute-start | bytes 589832 | tf_op jit(solution)/shard_map/ppermute | solution.py:291
  47.4 4.9 %collective-permute-start.6 = (f32[128,640]{1,0:T(8,128)S(1)}, f32[128,640]{1,0:T(8,128)S(1)}, u32[]{:S(2)}, u32[]{:S(2)}) collective-permute-start(f32[128,640]{1,0:T(8,128)S(1)} %collective-permute-done.4.got2), channel_id=1, source_target_pairs={{0,1},{1,0},{2,3},{3,2},{4,5},{5,4},{6,7},{7,6},{8,9},{9,8},{10,11... | collective-permute-start | bytes 983048 | tf_op jit(solution)/shard_map/ppermute | solution.py:268
  50.8 1.4 %collective-permute-start.7 = (f32[128,384]{1,0:T(8,128)S(1)}, f32[128,384]{1,0:T(8,128)S(1)}, u32[]{:S(2)}, u32[]{:S(2)}) collective-permute-start(f32[128,384]{1,0:T(8,128)S(1)} %collective-permute-done.5.got3), channel_id=1, source_target_pairs={{0,1},{1,0},{2,3},{3,2},{4,5},{5,4},{6,7},{7,6},{8,9},{9,8},{10,11... | collective-permute-start | bytes 589832 | tf_op jit(solution)/shard_map/ppermute | solution.py:268
  62.9 0.7 collective-permute-start.8
  63.6 2.2 %collective-permute-start.9 = (f32[256,640]{1,0:T(8,128)S(1)}, f32[256,640]{1,0:T(8,128)S(1)}, u32[]{:S(2)}, u32[]{:S(2)}) collective-permute-start(f32[256,640]{1,0:T(8,128)S(1)} %collective-permute-done.8.got), channel_id=1, source_target_pairs={{0,1},{1,0},{2,3},{3,2},{4,5},{5,4},{6,7},{7,6},{8,9},{9,8},{10,11... | collective-permute-start | bytes 1966088 | tf_op jit(solution)/shard_map/ppermute | solution.py:268
  85.2 26.9 %collective-permute-start.10 = (f32[384,128]{1,0:T(8,128)S(1)}, f32[384,128]{1,0:T(8,128)S(1)}, u32[]{:S(2)}, u32[]{:S(2)}) collective-permute-start(f32[384,128]{1,0:T(8,128)S(1)} %get-tuple-element.27), channel_id=1, source_target_pairs={{8,0},{16,24},{9,1},{17,25},{10,2},{18,26},{11,3},{19,27},{12,4},{... | collective-permute-start | bytes 589832 | tf_op jit(solution)/shard_map/ppermute | solution.py:316

commit v2 on v1

--- a/solution.py
+++ b/solution.py
@@ -91,6 +91,36 @@
         g[k : k + p, k + p :] = t
     for k in range(face - 2 * p, -1, -p):
         g[k : k + p, face:] -= dot(g[k : k + p, k + p : face], g[k + p : face, face:])
+
+
+def payload_blocks(count, p, s):
+    spots = [(r * p, c * p, p) for r in range(count) for c in range(r, count)]
+    return spots + [(r * p, -s, s) for r in range(count)]
+
+
+def pack(send_ref, n_ref, count, p):
+    half = p // 2
+    core = lax.axis_index("gy") % 2
+    width = n_ref.shape[1]
+    at = 0
+    for row, col, size in payload_blocks(count, p, width - n_ref.shape[0]):
+        col = col % width
+        rows = pl.ds(pl.multiple_of(row + core * half, half), half)
+        send_ref[:, at : at + size] = n_ref[rows, col : col + size]
+        at += size
+
+
+def unpack(q_ref, got, swapped, count, p):
+    half = p // 2
+    core = lax.axis_index("gy") % 2
+    width = q_ref.shape[1]
+    at = 0
+    for row, col, size in payload_blocks(count, p, width - q_ref.shape[0]):
+        col = col % width
+        for src, which in ((got, core), (swapped, 1 - core)):
+            rows = pl.ds(pl.multiple_of(row + which * half, half), half)
+            q_ref[rows, col : col + size] = src[:, at : at + size]
+        at += size
 
 
 def leaf_merge(own_map, own_flux, other_map, other_flux, n_ref, y_ref, send_ref, g):
@@ -145,18 +175,13 @@
             n_ref[i * p : (i + 1) * p, j * p : j * p + block.shape[1]] = block
     block_solve(g, p, p, n_ref)
     y_ref[...] = g[:, p:]
-    half = 3 * p // 2
-    mine = pl.ds(pl.multiple_of((gy % 2) * half, half), half)
-    send_ref[:, : 3 * p] = n_ref[mine, : 3 * p]
-    send_ref[:, 3 * p :] = n_ref[mine, 5 * p :]
-
-
-def column_merge(n0, got, swapped, n_ref, y_ref, send2_ref, send3_ref, g, q):
+    pack(send_ref, n_ref, 3, p)
+
+
+def column_merge(n0, got, swapped, n_ref, y_ref, send_ref, g, q):
     p = n0.shape[0] // 5
-    core = lax.axis_index("gy") % 2
-    half = 3 * p // 2
-    q[pl.ds(pl.multiple_of(core * half, half), half), :] = got[...]
-    q[pl.ds(pl.multiple_of((1 - core) * half, half), half), :] = swapped[...]
+    q[...] = jnp.zeros_like(q)
+    unpack(q, got, swapped, 3, p)
     f, o, e = 2 * p, 3 * p, 5 * p
     g[:, 0:f] = n0[0:f, 0:f] + q[0:f, 0:f]
     g[:, f : f + p] = n0[0:f, f:o]
@@ -172,41 +197,33 @@
     n_ref[2 * p :, 2 * p :] = n0[o:, o:]
     block_solve(g, f, p, n_ref)
     y_ref[...] = g[:, f:]
-    send2_ref[...] = n_ref[pl.ds(pl.multiple_of(core * p, p), p), :]
-    send3_ref[...] = n_ref[pl.ds(pl.multiple_of((2 + core) * p, p), p), 2 * p :]
-
-
-def row_merge(n1, got2, got3, swap2, swap3, n_ref, y_ref, send_ref, g, q2, q3):
+    pack(send_ref, n_ref, 4, p)
+
+
+def row_merge(n1, got, swapped, n_ref, y_ref, send_ref, g, q):
     p = n1.shape[0] // 4
-    core = lax.axis_index("gy") % 2
-    here = pl.ds(pl.multiple_of(core * p, p), p)
-    there = pl.ds(pl.multiple_of((1 - core) * p, p), p)
-    q2[here, :] = got2[...]
-    q2[there, :] = swap2[...]
-    q3[here, :] = got3[...]
-    q3[there, :] = swap3[...]
+    q[...] = jnp.zeros_like(q)
+    unpack(q, got, swapped, 4, p)
     f = 2 * p
-    g[:, 0:f] = n1[0:f, 0:f] + q2[:, 0:f]
+    g[:, 0:f] = n1[0:f, 0:f] + q[0:f, 0:f]
     g[:, f : 2 * f] = n1[0:f, f : 2 * f]
-    g[:, 2 * f : 3 * f] = q2[:, f : 2 * f]
-    g[:, 3 * f :] = n1[0:f, 2 * f :] + q2[:, 2 * f :]
+    g[:, 2 * f : 3 * f] = q[0:f, f : 2 * f]
+    g[:, 3 * f :] = n1[0:f, 2 * f :] + q[0:f, 2 * f :]
     n_ref[...] = jnp.zeros_like(n_ref)
     n_ref[0:f, 0:f] = n1[f:, f : 2 * f]
     n_ref[0:f, 2 * f :] = n1[f:, 2 * f :]
-    n_ref[f:, f:] = q3[...]
+    n_ref[f:, f:] = q[f:, f:]
     block_solve(g, f, p, n_ref)
     y_ref[...] = g[:, f:]
-    send_ref[...] = n_ref[pl.ds(pl.multiple_of(core * f, f), f), :]
+    pack(send_ref, n_ref, 4, p)
 
 
 def top_solve(n2, got, swapped, y2, y1, u_ref, send_ref, g):
     p = n2.shape[0] // 4
-    core = lax.axis_index("gy") % 2
     f = 2 * p
-    here = pl.ds(pl.multiple_of(core * f, f), f)
-    there = pl.ds(pl.multiple_of((1 - core) * f, f), f)
-    g[here, :] = n2[here, :] + got[...]
-    g[there, :] = n2[there, :] + swapped[...]
+    g[...] = jnp.zeros_like(g)
+    unpack(g, got, swapped, 4, p)
+    g[...] += n2[...]
     block_solve(g, 4 * p, p)
     u3 = -g[:, 4 * p :]
     u2 = -(dot(y2[:, : 4 * p], u3) + y2[:, 4 * p :])
@@ -271,7 +288,7 @@
     n0, y0, send = local(
         leaf_merge,
         "leaf_merge",
-        [(5 * p, 5 * p + s), (p, 5 * p + s), (3 * p // 2, 3 * p + s)],
+        [(5 * p, 5 * p + s), (p, 5 * p + s), (p // 2, 6 * p + 3 * s)],
         [(p, 6 * p + s)],
         own_map,
         own_flux,
@@ -279,27 +296,24 @@
         other_flux,
     )
     got = lax.ppermute(send, "gx", inward)
-    n1, y1, send2, send3 = local(
+    n1, y1, send = local(
         column_merge,
         "column_merge",
-        [(4 * p, 4 * p + s), (2 * p, 4 * p + s), (p, 4 * p + s), (p, 2 * p + s)],
+        [(4 * p, 4 * p + s), (2 * p, 4 * p + s), (p // 2, 10 * p + 4 * s)],
         [(2 * p, 6 * p + s), (3 * p, 3 * p + s)],
         n0,
         got,
         swap(got),
     )
-    got2, got3 = lax.ppermute((send2, send3), "gy", groups)
-    swap2, swap3 = swap((got2, got3))
+    got = lax.ppermute(send, "gy", groups)
     n2, y2, send = local(
         row_merge,
         "row_merge",
-        [(4 * p, 4 * p + s), (2 * p, 4 * p + s), (2 * p, 4 * p + s)],
-        [(2 * p, 6 * p + s), (2 * p, 4 * p + s), (2 * p, 2 * p + s)],
+        [(4 * p, 4 * p + s), (2 * p, 4 * p + s), (p // 2, 10 * p + 4 * s)],
+        [(2 * p, 6 * p + s), (4 * p, 4 * p + s)],
         n1,
-        got2,
-        got3,
-        swap2,
-        swap3,
+        got,
+        swap(got),
     )
     got = lax.ppermute(send, "gx", across)
     u, send = local(

time: 114 us -> 106 us (0.930)
  waiting for transfers between devices: 53.9 us -> 46.7 us
    ppermute x1, waiting for transfers between devices: 25.6 us -> 21.3 us  [shards(): got = lax.ppermute(send, 'gx', outward)]
    ppermute x1, waiting for transfers between devices: 8.45 us -> 6.35 us  [shards(): got = lax.ppermute(send, 'gx', inward)]
    ppermute x2 -> x1, waiting for transfers between devices: 11.9 us -> 11.1 us  [shards(): got = lax.ppermute(send, 'gy', groups)]
    ppermute x6 -> x5, waiting for transfers between devices: 7.93 us -> 7.89 us  [swap(): return lax.ppermute(x, 'gy', cores)]
  transfers between devices with their start and end apart: 11 -> 9, of which waited for: 8 -> 7; matrix products, arithmetic and copies ran while one was open for 0% -> 0% of each run, Pallas kernels for 0% -> 0%
where the time goes in v2:
time: 106 us
  Pallas kernels  47.4 us (45%)
  waiting for transfers between devices  46.7 us (44%)
  starting transfers between devices  9.31 us (9%)
  local copies, waits for them, and re-layouts  2.17 us (2%)
    pallas_call x5, Pallas kernels, local(): pl.pallas_call(kernel, name=name, out_shape=[jax.ShapeDtypeStruct(shape,...  47.4 us
    ppermute x1, waiting for transfers between devices, shards(): got = lax.ppermute(send, 'gx', outward)  21.3 us
    ppermute x1, waiting for transfers between devices, shards(): got = lax.ppermute(send, 'gy', groups)  11.1 us
    ppermute x5, waiting for transfers between devices, swap(): return lax.ppermute(x, 'gy', cores)  7.89 us
    ppermute x1, waiting for transfers between devices, shards(): got = lax.ppermute(send, 'gx', inward)  6.35 us
    ppermute x1, starting transfers between devices, shards(): got = lax.ppermute(send, 'gx', inward)  5.04 us
    unnamed x4, local copies, waits for them, and re-layouts  2.17 us
  transfers between devices with their start and end apart: 9, of which 7 were waited for; matrix products, arithmetic and copies ran while one was open for 0% of the time, Pallas kernels for 0%

profile of v2, /device:TPU:0, one launch (start us, length us, event | category | flops | bytes accessed | tf_op | source)
XLA Modules:
  0.0 105.6 jit_solution(15896946030278275378)
XLA Ops:
  0.0 0.5 collective-permute-start
  0.5 0.1 collective-permute-start.1
  0.5 2.8 %collective-permute-done.1.other_flux = f32[512,128]{1,0:T(8,128)S(1)} collective-permute-done((f32[512,128]{1,0:T(8,128)}, f32[512,128]{1,0:T(8,128)S(1)}, u32[]{:S(2)}, u32[]{:S(2)}) %collective-permute-start.1) | collective-permute-done | bytes 262176 | tf_op jit(solution)/shard_map/ppermute | solution.py:285
  3.3 0.0 collective-permute-done.other_map
  3.3 1.2 %copy-done = f32[1,1,512,512]{3,2,1,0:T(8,128)S(1)} copy-done((f32[1,1,512,512]{3,2,1,0:T(8,128)S(1)}, f32[1,1,512,512]{3,2,1,0:T(8,128)}, u32[]{:S(2)}) %copy-start) | copy-done | bytes 1048600
  4.6 0.9 copy-done.1
  5.5 5.7 %leaf_merge.1 = (f32[640,768]{1,0:T(8,128)S(1)}, f32[128,768]{1,0:T(8,128)S(1)}, f32[64,1152]{1,0:T(8,128)S(1)}) custom-call(f32[512,512]{1,0:T(8,128)S(1)} %bitcast.4, f32[512,128]{1,0:T(8,128)S(1)} %bitcast.6, f32[512,512]{1,0:T(8,128)S(1)} %collective-permute-done.other_map, f32[512,128]{1,0:T(8,128)S(1)} %collective-permute-done.1.other_flux), custom_call_target="tpu_custom_call" | custom-call | tf_op jit(solution)/shard_map/leaf_merge/pallas_call | solution.py:261
  11.2 5.0 %collective-permute-start.2 = (f32[64,1152]{1,0:T(8,128)S(1)}, f32[64,1152]{1,0:T(8,128)S(1)}, u32[]{:S(2)}, u32[]{:S(2)}) collective-permute-start(f32[64,1152]{1,0:T(8,128)S(1)} %get-tuple-element.17), channel_id=1, source_target_pairs={{0,8},{24,16},{1,9},{25,17},{2,10},{26,18},{3,11},{27,19},{4,12},{... | collective-permute-start | bytes 884744 | tf_op jit(solution)/shard_map/ppermute | solution.py:298
  16.2 6.4 %collective-permute-done.2.got = f32[64,1152]{1,0:T(8,128)S(1)} collective-permute-done((f32[64,1152]{1,0:T(8,128)S(1)}, f32[64,1152]{1,0:T(8,128)S(1)}, u32[]{:S(2)}, u32[]{:S(2)}) %collective-permute-start.2) | collective-permute-done | bytes 294944 | tf_op jit(solution)/shard_map/ppermute | solution.py:298
  22.6 0.0 collective-permute-start.3
  22.6 1.6 %collective-permute-done.3.swapped = f32[64,1152]{1,0:T(8,128)S(1)} collective-permute-done((f32[64,1152]{1,0:T(8,128)S(1)}, f32[64,1152]{1,0:T(8,128)S(1)}, u32[]{:S(2)}, u32[]{:S(2)}) %collective-permute-start.3) | collective-permute-done | bytes 294944 | tf_op jit(solution)/shard_map/ppermute | solution.py:285
  24.2 10.4 %column_merge.1 = (f32[512,640]{1,0:T(8,128)S(1)}, f32[256,640]{1,0:T(8,128)S(1)}, f32[64,1792]{1,0:T(8,128)S(1)}) custom-call(f32[640,768]{1,0:T(8,128)S(1)} %get-tuple-element.16.n0, f32[64,1152]{1,0:T(8,128)S(1)} %collective-permute-done.2.got, f32[64,1152]{1,0:T(8,128)S(1)} %collective-permute-done.3.swapped), custom_call_target="tpu_custom_call" | custom-call | tf_op jit(solution)/shard_map/column_merge/pallas_call | solution.py:261
  34.5 1.6 %collective-permute-start.4 = (f32[64,1792]{1,0:T(8,128)S(1)}, f32[64,1792]{1,0:T(8,128)S(1)}, u32[]{:S(2)}, u32[]{:S(2)}) collective-permute-start(f32[64,1792]{1,0:T(8,128)S(1)} %get-tuple-element.19), channel_id=1, source_target_pairs={{0,2},{1,3},{2,0},{3,1},{4,6},{5,7},{6,4},{7,5},{8,10},{9,11},{10,... | collective-permute-start | bytes 1376264 | tf_op jit(solution)/shard_map/ppermute | solution.py:308
  36.1 11.1 %collective-permute-done.4.got = f32[64,1792]{1,0:T(8,128)S(1)} collective-permute-done((f32[64,1792]{1,0:T(8,128)S(1)}, f32[64,1792]{1,0:T(8,128)S(1)}, u32[]{:S(2)}, u32[]{:S(2)}) %collective-permute-start.4) | collective-permute-done | bytes 458784 | tf_op jit(solution)/shard_map/ppermute | solution.py:308
  47.2 0.0 collective-permute-start.5
  47.2 1.8 %collective-permute-done.5.swapped = f32[64,1792]{1,0:T(8,128)S(1)} collective-permute-done((f32[64,1792]{1,0:T(8,128)S(1)}, f32[64,1792]{1,0:T(8,128)S(1)}, u32[]{:S(2)}, u32[]{:S(2)}) %collective-permute-start.5) | collective-permute-done | bytes 458784 | tf_op jit(solution)/shard_map/ppermute | solution.py:285
  49.0 10.6 %row_merge.1 = (f32[512,640]{1,0:T(8,128)S(1)}, f32[256,640]{1,0:T(8,128)S(1)}, f32[64,1792]{1,0:T(8,128)S(1)}) custom-call(f32[512,640]{1,0:T(8,128)S(1)} %get-tuple-element.18.n1, f32[64,1792]{1,0:T(8,128)S(1)} %collective-permute-done.4.got, f32[64,1792]{1,0:T(8,128)S(1)} %collective-permute-done.5.swapped), custom_call_target="tpu_custom_call" | custom-call | tf_op jit(solution)/shard_map/row_merge/pallas_call | solution.py:261
  59.6 0.7 collective-permute-start.6
  60.3 0.2 collective-permute-start.7
  60.6 1.7 %collective-permute-done.7.swapped = f32[64,1792]{1,0:T(8,128)S(1)} collective-permute-done((f32[64,1792]{1,0:T(8,128)S(1)}, f32[64,1792]{1,0:T(8,128)S(1)}, u32[]{:S(2)}, u32[]{:S(2)}) %collective-permute-start.7) | collective-permute-done | bytes 458784 | tf_op jit(solution)/shard_map/ppermute | solution.py:285
  62.2 19.5 %top_solve.1 = (f32[640,128]{1,0:T(8,128)S(1)}, f32[384,128]{1,0:T(8,128)S(1)}) custom-call(f32[512,640]{1,0:T(8,128)S(1)} %get-tuple-element.20.n2, f32[64,1792]{1,0:T(8,128)S(1)} %collective-permute-done.6.got, f32[64,1792]{1,0:T(8,128)S(1)} %collective-permute-done.7.swapped, f32[256,640]{1,0:T(8,128)S(1)} %get-tuple-element.22.y2, ...), custom_call_target="tpu_custom_call" | custom-call | tf_op jit(solution)/shard_map/top_solve/pallas_call | solution.py:261
  81.8 1.3 %collective-permute-start.8 = (f32[384,128]{1,0:T(8,128)S(1)}, f32[384,128]{1,0:T(8,128)S(1)}, u32[]{:S(2)}, u32[]{:S(2)}) collective-permute-start(f32[384,128]{1,0:T(8,128)S(1)} %get-tuple-element.25), channel_id=1, source_target_pairs={{8,0},{16,24},{9,1},{17,25},{10,2},{18,26},{11,3},{19,27},{12,4},{... | collective-permute-start | bytes 589832 | tf_op jit(solution)/shard_map/ppermute | solution.py:330
  83.1 21.3 %collective-permute-done.8.got = f32[384,128]{1,0:T(8,128)S(1)} collective-permute-done((f32[384,128]{1,0:T(8,128)S(1)}, f32[384,128]{1,0:T(8,128)S(1)}, u32[]{:S(2)}, u32[]{:S(2)}) %collective-permute-start.8) | collective-permute-done | bytes 196640 | tf_op jit(solution)/shard_map/ppermute | solution.py:330
  104.4 1.2 %leaf_values.1 = f32[512,128]{1,0:T(8,128)} custom-call(f32[640,128]{1,0:T(8,128)S(1)} %get-tuple-element.24.own, f32[384,128]{1,0:T(8,128)S(1)} %collective-permute-done.8.got, f32[128,768]{1,0:T(8,128)S(1)} %get-tuple-element.26.y0), custom_call_target="tpu_custom_call" | custom-call | tf_op jit(solution)/shard_map/leaf_values/pallas_call | solution.py:261
  (3 shorter events, 0.0 us)
Async XLA Ops:
  0.0 3.3 %collective-permute-start = (f32[512,512]{1,0:T(8,128)}, f32[512,512]{1,0:T(8,128)S(1)}, u32[]{:S(2)}, u32[]{:S(2)}) collective-permute-start(f32[512,512]{1,0:T(8,128)} %bitcast.3), channel_id=1, source_target_pairs={{0,1},{1,0},{2,3},{3,2},{4,5},{5,4},{6,7},{7,6},{8,9},{9,8},{10,11... | collective-permute-start | bytes 3145736 | tf_op jit(solution)/shard_map/ppermute | solution.py:285
  0.5 2.9 %collective-permute-start.1 = (f32[512,128]{1,0:T(8,128)}, f32[512,128]{1,0:T(8,128)S(1)}, u32[]{:S(2)}, u32[]{:S(2)}) collective-permute-start(f32[512,128]{1,0:T(8,128)} %bitcast.5), channel_id=1, source_target_pairs={{0,1},{1,0},{2,3},{3,2},{4,5},{5,4},{6,7},{7,6},{8,9},{9,8},{10,11... | collective-permute-start | bytes 786440 | tf_op jit(solution)/shard_map/ppermute | solution.py:285
  3.3 1.2 %copy-start = (f32[1,1,512,512]{3,2,1,0:T(8,128)S(1)}, f32[1,1,512,512]{3,2,1,0:T(8,128)}, u32[]{:S(2)}) copy-start(f32[1,1,512,512]{3,2,1,0:T(8,128)} %param.2) | copy-start | bytes 3145732
  4.6 0.9 copy-start.1
  11.2 11.4 %collective-permute-start.2 = (f32[64,1152]{1,0:T(8,128)S(1)}, f32[64,1152]{1,0:T(8,128)S(1)}, u32[]{:S(2)}, u32[]{:S(2)}) collective-permute-start(f32[64,1152]{1,0:T(8,128)S(1)} %get-tuple-element.17), channel_id=1, source_target_pairs={{0,8},{24,16},{1,9},{25,17},{2,10},{26,18},{3,11},{27,19},{4,12},{... | collective-permute-start | bytes 884744 | tf_op jit(solution)/shard_map/ppermute | solution.py:298
  22.6 1.6 %collective-permute-start.3 = (f32[64,1152]{1,0:T(8,128)S(1)}, f32[64,1152]{1,0:T(8,128)S(1)}, u32[]{:S(2)}, u32[]{:S(2)}) collective-permute-start(f32[64,1152]{1,0:T(8,128)S(1)} %collective-permute-done.2.got), channel_id=1, source_target_pairs={{0,1},{1,0},{2,3},{3,2},{4,5},{5,4},{6,7},{7,6},{8,9},{9,8},{10,11... | collective-permute-start | bytes 884744 | tf_op jit(solution)/shard_map/ppermute | solution.py:285
  34.5 12.6 %collective-permute-start.4 = (f32[64,1792]{1,0:T(8,128)S(1)}, f32[64,1792]{1,0:T(8,128)S(1)}, u32[]{:S(2)}, u32[]{:S(2)}) collective-permute-start(f32[64,1792]{1,0:T(8,128)S(1)} %get-tuple-element.19), channel_id=1, source_target_pairs={{0,2},{1,3},{2,0},{3,1},{4,6},{5,7},{6,4},{7,5},{8,10},{9,11},{10,... | collective-permute-start | bytes 1376264 | tf_op jit(solution)/shard_map/ppermute | solution.py:308
  47.2 1.8 %collective-permute-start.5 = (f32[64,1792]{1,0:T(8,128)S(1)}, f32[64,1792]{1,0:T(8,128)S(1)}, u32[]{:S(2)}, u32[]{:S(2)}) collective-permute-start(f32[64,1792]{1,0:T(8,128)S(1)} %collective-permute-done.4.got), channel_id=1, source_target_pairs={{0,1},{1,0},{2,3},{3,2},{4,5},{5,4},{6,7},{7,6},{8,9},{9,8},{10,11... | collective-permute-start | bytes 1376264 | tf_op jit(solution)/shard_map/ppermute | solution.py:285
  59.6 0.7 collective-permute-start.6
  60.3 1.9 %collective-permute-start.7 = (f32[64,1792]{1,0:T(8,128)S(1)}, f32[64,1792]{1,0:T(8,128)S(1)}, u32[]{:S(2)}, u32[]{:S(2)}) collective-permute-start(f32[64,1792]{1,0:T(8,128)S(1)} %collective-permute-done.6.got), channel_id=1, source_target_pairs={{0,1},{1,0},{2,3},{3,2},{4,5},{5,4},{6,7},{7,6},{8,9},{9,8},{10,11... | collective-permute-start | bytes 1376264 | tf_op jit(solution)/shard_map/ppermute | solution.py:285
  81.8 22.6 %collective-permute-start.8 = (f32[384,128]{1,0:T(8,128)S(1)}, f32[384,128]{1,0:T(8,128)S(1)}, u32[]{:S(2)}, u32[]{:S(2)}) collective-permute-start(f32[384,128]{1,0:T(8,128)S(1)} %get-tuple-element.25), channel_id=1, source_target_pairs={{8,0},{16,24},{9,1},{17,25},{10,2},{18,26},{11,3},{19,27},{12,4},{... | collective-permute-start | bytes 589832 | tf_op jit(solution)/shard_map/ppermute | solution.py:330

commit v3 on v2

--- a/solution.py
+++ b/solution.py
@@ -80,17 +80,30 @@
 
 
 def block_solve(g, face, p, schur=None):
+    pivot = g[0:p, 0:p]
     for k in range(0, face, p):
         head = g[k : k + p, k + p :]
-        t = dot(spd_inverse(g[k : k + p, k : k + p]), head)
+        t = dot(spd_inverse(pivot), head)
         if k + p < face:
+            after = slice(k + p, k + 2 * p)
+            pivot = g[after, after] - tdot(head[:, :p], t[:, :p])
             g[k + p : face, k + p :] -= tdot(head[:, : face - k - p], t)
         if schur is not None:
             outer = head[:, face - k - p : face - k - p + schur.shape[0]]
             schur[...] -= tdot(outer, t[:, face - k - p :])
         g[k : k + p, k + p :] = t
+
+
+def face_values(g, outer, p):
+    face = g.shape[0]
+    rest = g[:, face:] if outer is None else g[:, face + outer.shape[0] :]
+    if outer is not None:
+        rest = rest + dot(g[:, face : face + outer.shape[0]], outer)
+    found = -rest[face - p :]
     for k in range(face - 2 * p, -1, -p):
-        g[k : k + p, face:] -= dot(g[k : k + p, k + p : face], g[k + p : face, face:])
+        here = -rest[k : k + p] - dot(g[k : k + p, k + p : face], found)
+        found = jnp.concatenate([here, found], axis=0)
+    return found
 
 
 def payload_blocks(count, p, s):
@@ -178,7 +191,7 @@
     pack(send_ref, n_ref, 3, p)
 
 
-def column_merge(n0, got, swapped, n_ref, y_ref, send_ref, g, q):
+def column_merge(n0, got, swapped, n_ref, g, send_ref, q):
     p = n0.shape[0] // 5
     q[...] = jnp.zeros_like(q)
     unpack(q, got, swapped, 3, p)
@@ -196,11 +209,10 @@
     n_ref[2 * p :, 0:p] = n0[o:, f:o]
     n_ref[2 * p :, 2 * p :] = n0[o:, o:]
     block_solve(g, f, p, n_ref)
-    y_ref[...] = g[:, f:]
     pack(send_ref, n_ref, 4, p)
 
 
-def row_merge(n1, got, swapped, n_ref, y_ref, send_ref, g, q):
+def row_merge(n1, got, swapped, n_ref, g, send_ref, q):
     p = n1.shape[0] // 4
     q[...] = jnp.zeros_like(q)
     unpack(q, got, swapped, 4, p)
@@ -214,7 +226,6 @@
     n_ref[0:f, 2 * f :] = n1[f:, 2 * f :]
     n_ref[f:, f:] = q[f:, f:]
     block_solve(g, f, p, n_ref)
-    y_ref[...] = g[:, f:]
     pack(send_ref, n_ref, 4, p)
 
 
@@ -225,11 +236,11 @@
     unpack(g, got, swapped, 4, p)
     g[...] += n2[...]
     block_solve(g, 4 * p, p)
-    u3 = -g[:, 4 * p :]
-    u2 = -(dot(y2[:, : 4 * p], u3) + y2[:, 4 * p :])
+    u3 = face_values(g, None, p)
+    u2 = face_values(y2, u3, p)
     u_ref[3 * p :, :] = u3[0:f]
     group = jnp.concatenate([u2, u3[0:f]], axis=0)
-    u1 = -(dot(y1[:, : 4 * p], group) + y1[:, 4 * p :])
+    u1 = face_values(y1, group, p)
     u_ref[0:f, :] = u1
     u_ref[f : 3 * p, :] = u2[0:p]
     send_ref[0:f, :] = u1
@@ -299,8 +310,8 @@
     n1, y1, send = local(
         column_merge,
         "column_merge",
-        [(4 * p, 4 * p + s), (2 * p, 4 * p + s), (p // 2, 10 * p + 4 * s)],
-        [(2 * p, 6 * p + s), (3 * p, 3 * p + s)],
+        [(4 * p, 4 * p + s), (2 * p, 6 * p + s), (p // 2, 10 * p + 4 * s)],
+        [(3 * p, 3 * p + s)],
         n0,
         got,
         swap(got),
@@ -309,8 +320,8 @@
     n2, y2, send = local(
         row_merge,
         "row_merge",
-        [(4 * p, 4 * p + s), (2 * p, 4 * p + s), (p // 2, 10 * p + 4 * s)],
-        [(2 * p, 6 * p + s), (4 * p, 4 * p + s)],
+        [(4 * p, 4 * p + s), (2 * p, 6 * p + s), (p // 2, 10 * p + 4 * s)],
+        [(4 * p, 4 * p + s)],
         n1,
         got,
         swap(got),

time: 106 us -> 105 us (level)
  Pallas kernels: 47.4 us -> 46.2 us
    pallas_call x5, Pallas kernels: 47.4 us -> 46.2 us  [local(): pl.pallas_call(kernel, name=name, out_shape=[jax.ShapeDtypeStruct(shape,...]
where the time goes in v3:
time: 105 us; the launch traced here: 104 us
  waiting for transfers between devices  46.4 us (44%)
  Pallas kernels  46.2 us (44%)
  starting transfers between devices  9.53 us (9%)
  local copies, waits for them, and re-layouts  2.17 us (2%)
    pallas_call x5, Pallas kernels, local(): pl.pallas_call(kernel, name=name, out_shape=[jax.ShapeDtypeStruct(shape,...  46.2 us
    ppermute x1, waiting for transfers between devices, shards(): got = lax.ppermute(send, 'gx', outward)  21.1 us
    ppermute x1, waiting for transfers between devices, shards(): got = lax.ppermute(send, 'gy', groups)  11.1 us
    ppermute x5, waiting for transfers between devices, swap(): return lax.ppermute(x, 'gy', cores)  7.89 us
    ppermute x1, waiting for transfers between devices, shards(): got = lax.ppermute(send, 'gx', inward)  6.35 us
    ppermute x1, starting transfers between devices, shards(): got = lax.ppermute(send, 'gx', inward)  5.04 us
    unnamed x4, local copies, waits for them, and re-layouts  2.17 us
  transfers between devices with their start and end apart: 9, of which 7 were waited for; matrix products, arithmetic and copies ran while one was open for 0% of the time, Pallas kernels for 0%

profile of v3, /device:TPU:0, one launch (start us, length us, event | category | flops | bytes accessed | tf_op | source)
XLA Modules:
  0.0 104.4 jit_solution(13665792675462808831)
XLA Ops:
  0.0 0.5 collective-permute-start
  0.5 0.1 collective-permute-start.1
  0.5 2.8 %collective-permute-done.1.other_flux = f32[512,128]{1,0:T(8,128)S(1)} collective-permute-done((f32[512,128]{1,0:T(8,128)}, f32[512,128]{1,0:T(8,128)S(1)}, u32[]{:S(2)}, u32[]{:S(2)}) %collective-permute-start.1) | collective-permute-done | bytes 262176 | tf_op jit(solution)/shard_map/ppermute | solution.py:296
  3.3 0.0 collective-permute-done.other_map
  3.3 1.2 %copy-done = f32[1,1,512,512]{3,2,1,0:T(8,128)S(1)} copy-done((f32[1,1,512,512]{3,2,1,0:T(8,128)S(1)}, f32[1,1,512,512]{3,2,1,0:T(8,128)}, u32[]{:S(2)}) %copy-start) | copy-done | bytes 1048600
  4.6 0.9 copy-done.1
  5.5 5.7 %leaf_merge.1 = (f32[640,768]{1,0:T(8,128)S(1)}, f32[128,768]{1,0:T(8,128)S(1)}, f32[64,1152]{1,0:T(8,128)S(1)}) custom-call(f32[512,512]{1,0:T(8,128)S(1)} %bitcast.4, f32[512,128]{1,0:T(8,128)S(1)} %bitcast.6, f32[512,512]{1,0:T(8,128)S(1)} %collective-permute-done.other_map, f32[512,128]{1,0:T(8,128)S(1)} %collective-permute-done.1.other_flux), custom_call_target="tpu_custom_call" | custom-call | tf_op jit(solution)/shard_map/leaf_merge/pallas_call | solution.py:272
  11.2 5.0 %collective-permute-start.2 = (f32[64,1152]{1,0:T(8,128)S(1)}, f32[64,1152]{1,0:T(8,128)S(1)}, u32[]{:S(2)}, u32[]{:S(2)}) collective-permute-start(f32[64,1152]{1,0:T(8,128)S(1)} %get-tuple-element.17), channel_id=1, source_target_pairs={{0,8},{24,16},{1,9},{25,17},{2,10},{26,18},{3,11},{27,19},{4,12},{... | collective-permute-start | bytes 884744 | tf_op jit(solution)/shard_map/ppermute | solution.py:309
  16.2 6.4 %collective-permute-done.2.got = f32[64,1152]{1,0:T(8,128)S(1)} collective-permute-done((f32[64,1152]{1,0:T(8,128)S(1)}, f32[64,1152]{1,0:T(8,128)S(1)}, u32[]{:S(2)}, u32[]{:S(2)}) %collective-permute-start.2) | collective-permute-done | bytes 294944 | tf_op jit(solution)/shard_map/ppermute | solution.py:309
  22.6 1.6 %collective-permute-done.3.swapped = f32[64,1152]{1,0:T(8,128)S(1)} collective-permute-done((f32[64,1152]{1,0:T(8,128)S(1)}, f32[64,1152]{1,0:T(8,128)S(1)}, u32[]{:S(2)}, u32[]{:S(2)}) %collective-permute-start.3) | collective-permute-done | bytes 294944 | tf_op jit(solution)/shard_map/ppermute | solution.py:296
  24.2 10.3 %column_merge.1 = (f32[512,640]{1,0:T(8,128)S(1)}, f32[256,896]{1,0:T(8,128)S(1)}, f32[64,1792]{1,0:T(8,128)S(1)}) custom-call(f32[640,768]{1,0:T(8,128)S(1)} %get-tuple-element.16.n0, f32[64,1152]{1,0:T(8,128)S(1)} %collective-permute-done.2.got, f32[64,1152]{1,0:T(8,128)S(1)} %collective-permute-done.3.swapped), custom_call_target="tpu_custom_call" | custom-call | tf_op jit(solution)/shard_map/column_merge/pallas_call | solution.py:272
  34.5 1.6 %collective-permute-start.4 = (f32[64,1792]{1,0:T(8,128)S(1)}, f32[64,1792]{1,0:T(8,128)S(1)}, u32[]{:S(2)}, u32[]{:S(2)}) collective-permute-start(f32[64,1792]{1,0:T(8,128)S(1)} %get-tuple-element.19), channel_id=1, source_target_pairs={{0,2},{1,3},{2,0},{3,1},{4,6},{5,7},{6,4},{7,5},{8,10},{9,11},{10,... | collective-permute-start | bytes 1376264 | tf_op jit(solution)/shard_map/ppermute | solution.py:319
  36.0 11.1 %collective-permute-done.4.got = f32[64,1792]{1,0:T(8,128)S(1)} collective-permute-done((f32[64,1792]{1,0:T(8,128)S(1)}, f32[64,1792]{1,0:T(8,128)S(1)}, u32[]{:S(2)}, u32[]{:S(2)}) %collective-permute-start.4) | collective-permute-done | bytes 458784 | tf_op jit(solution)/shard_map/ppermute | solution.py:319
  47.1 0.0 collective-permute-start.5
  47.1 1.8 %collective-permute-done.5.swapped = f32[64,1792]{1,0:T(8,128)S(1)} collective-permute-done((f32[64,1792]{1,0:T(8,128)S(1)}, f32[64,1792]{1,0:T(8,128)S(1)}, u32[]{:S(2)}, u32[]{:S(2)}) %collective-permute-start.5) | collective-permute-done | bytes 458784 | tf_op jit(solution)/shard_map/ppermute | solution.py:296
  48.9 10.3 %row_merge.1 = (f32[512,640]{1,0:T(8,128)S(1)}, f32[256,896]{1,0:T(8,128)S(1)}, f32[64,1792]{1,0:T(8,128)S(1)}) custom-call(f32[512,640]{1,0:T(8,128)S(1)} %get-tuple-element.18.n1, f32[64,1792]{1,0:T(8,128)S(1)} %collective-permute-done.4.got, f32[64,1792]{1,0:T(8,128)S(1)} %collective-permute-done.5.swapped), custom_call_target="tpu_custom_call" | custom-call | tf_op jit(solution)/shard_map/row_merge/pallas_call | solution.py:272
  59.2 0.9 collective-permute-start.6
  60.1 0.0 collective-permute-done.6.got
  60.1 0.2 collective-permute-start.7
  60.3 1.7 %collective-permute-done.7.swapped = f32[64,1792]{1,0:T(8,128)S(1)} collective-permute-done((f32[64,1792]{1,0:T(8,128)S(1)}, f32[64,1792]{1,0:T(8,128)S(1)}, u32[]{:S(2)}, u32[]{:S(2)}) %collective-permute-start.7) | collective-permute-done | bytes 458784 | tf_op jit(solution)/shard_map/ppermute | solution.py:296
  62.0 18.8 %top_solve.1 = (f32[640,128]{1,0:T(8,128)S(1)}, f32[384,128]{1,0:T(8,128)S(1)}) custom-call(f32[512,640]{1,0:T(8,128)S(1)} %get-tuple-element.20.n2, f32[64,1792]{1,0:T(8,128)S(1)} %collective-permute-done.6.got, f32[64,1792]{1,0:T(8,128)S(1)} %collective-permute-done.7.swapped, f32[256,896]{1,0:T(8,128)S(1)} %get-tuple-element.22.y2, ...), custom_call_target="tpu_custom_call" | custom-call | tf_op jit(solution)/shard_map/top_solve/pallas_call | solution.py:272
  80.8 1.3 %collective-permute-start.8 = (f32[384,128]{1,0:T(8,128)S(1)}, f32[384,128]{1,0:T(8,128)S(1)}, u32[]{:S(2)}, u32[]{:S(2)}) collective-permute-start(f32[384,128]{1,0:T(8,128)S(1)} %get-tuple-element.25), channel_id=1, source_target_pairs={{8,0},{16,24},{9,1},{17,25},{10,2},{18,26},{11,3},{19,27},{12,4},{... | collective-permute-start | bytes 589832 | tf_op jit(solution)/shard_map/ppermute | solution.py:341
  82.1 21.1 %collective-permute-done.8.got = f32[384,128]{1,0:T(8,128)S(1)} collective-permute-done((f32[384,128]{1,0:T(8,128)S(1)}, f32[384,128]{1,0:T(8,128)S(1)}, u32[]{:S(2)}, u32[]{:S(2)}) %collective-permute-start.8) | collective-permute-done | bytes 196640 | tf_op jit(solution)/shard_map/ppermute | solution.py:341
  103.2 1.2 %leaf_values.1 = f32[512,128]{1,0:T(8,128)} custom-call(f32[640,128]{1,0:T(8,128)S(1)} %get-tuple-element.24.own, f32[384,128]{1,0:T(8,128)S(1)} %collective-permute-done.8.got, f32[128,768]{1,0:T(8,128)S(1)} %get-tuple-element.26.y0), custom_call_target="tpu_custom_call" | custom-call | tf_op jit(solution)/shard_map/leaf_values/pallas_call | solution.py:272
  (3 shorter events, 0.0 us)
Async XLA Ops:
  0.0 3.3 %collective-permute-start = (f32[512,512]{1,0:T(8,128)}, f32[512,512]{1,0:T(8,128)S(1)}, u32[]{:S(2)}, u32[]{:S(2)}) collective-permute-start(f32[512,512]{1,0:T(8,128)} %bitcast.3), channel_id=1, source_target_pairs={{0,1},{1,0},{2,3},{3,2},{4,5},{5,4},{6,7},{7,6},{8,9},{9,8},{10,11... | collective-permute-start | bytes 3145736 | tf_op jit(solution)/shard_map/ppermute | solution.py:296
  0.5 2.9 %collective-permute-start.1 = (f32[512,128]{1,0:T(8,128)}, f32[512,128]{1,0:T(8,128)S(1)}, u32[]{:S(2)}, u32[]{:S(2)}) collective-permute-start(f32[512,128]{1,0:T(8,128)} %bitcast.5), channel_id=1, source_target_pairs={{0,1},{1,0},{2,3},{3,2},{4,5},{5,4},{6,7},{7,6},{8,9},{9,8},{10,11... | collective-permute-start | bytes 786440 | tf_op jit(solution)/shard_map/ppermute | solution.py:296
  3.3 1.2 %copy-start = (f32[1,1,512,512]{3,2,1,0:T(8,128)S(1)}, f32[1,1,512,512]{3,2,1,0:T(8,128)}, u32[]{:S(2)}) copy-start(f32[1,1,512,512]{3,2,1,0:T(8,128)} %param.2) | copy-start | bytes 3145732
  4.6 0.9 copy-start.1
  11.2 11.4 %collective-permute-start.2 = (f32[64,1152]{1,0:T(8,128)S(1)}, f32[64,1152]{1,0:T(8,128)S(1)}, u32[]{:S(2)}, u32[]{:S(2)}) collective-permute-start(f32[64,1152]{1,0:T(8,128)S(1)} %get-tuple-element.17), channel_id=1, source_target_pairs={{0,8},{24,16},{1,9},{25,17},{2,10},{26,18},{3,11},{27,19},{4,12},{... | collective-permute-start | bytes 884744 | tf_op jit(solution)/shard_map/ppermute | solution.py:309
  22.6 1.6 %collective-permute-start.3 = (f32[64,1152]{1,0:T(8,128)S(1)}, f32[64,1152]{1,0:T(8,128)S(1)}, u32[]{:S(2)}, u32[]{:S(2)}) collective-permute-start(f32[64,1152]{1,0:T(8,128)S(1)} %collective-permute-done.2.got), channel_id=1, source_target_pairs={{0,1},{1,0},{2,3},{3,2},{4,5},{5,4},{6,7},{7,6},{8,9},{9,8},{10,11... | collective-permute-start | bytes 884744 | tf_op jit(solution)/shard_map/ppermute | solution.py:296
  34.5 12.6 %collective-permute-start.4 = (f32[64,1792]{1,0:T(8,128)S(1)}, f32[64,1792]{1,0:T(8,128)S(1)}, u32[]{:S(2)}, u32[]{:S(2)}) collective-permute-start(f32[64,1792]{1,0:T(8,128)S(1)} %get-tuple-element.19), channel_id=1, source_target_pairs={{0,2},{1,3},{2,0},{3,1},{4,6},{5,7},{6,4},{7,5},{8,10},{9,11},{10,... | collective-permute-start | bytes 1376264 | tf_op jit(solution)/shard_map/ppermute | solution.py:319
  47.1 1.8 %collective-permute-start.5 = (f32[64,1792]{1,0:T(8,128)S(1)}, f32[64,1792]{1,0:T(8,128)S(1)}, u32[]{:S(2)}, u32[]{:S(2)}) collective-permute-start(f32[64,1792]{1,0:T(8,128)S(1)} %collective-permute-done.4.got), channel_id=1, source_target_pairs={{0,1},{1,0},{2,3},{3,2},{4,5},{5,4},{6,7},{7,6},{8,9},{9,8},{10,11... | collective-permute-start | bytes 1376264 | tf_op jit(solution)/shard_map/ppermute | solution.py:296
  59.2 0.9 collective-permute-start.6
  60.1 1.9 %collective-permute-start.7 = (f32[64,1792]{1,0:T(8,128)S(1)}, f32[64,1792]{1,0:T(8,128)S(1)}, u32[]{:S(2)}, u32[]{:S(2)}) collective-permute-start(f32[64,1792]{1,0:T(8,128)S(1)} %collective-permute-done.6.got), channel_id=1, source_target_pairs={{0,1},{1,0},{2,3},{3,2},{4,5},{5,4},{6,7},{7,6},{8,9},{9,8},{10,11... | collective-permute-start | bytes 1376264 | tf_op jit(solution)/shard_map/ppermute | solution.py:296
  80.8 22.4 %collective-permute-start.8 = (f32[384,128]{1,0:T(8,128)S(1)}, f32[384,128]{1,0:T(8,128)S(1)}, u32[]{:S(2)}, u32[]{:S(2)}) collective-permute-start(f32[384,128]{1,0:T(8,128)S(1)} %get-tuple-element.25), channel_id=1, source_target_pairs={{8,0},{16,24},{9,1},{17,25},{10,2},{18,26},{11,3},{19,27},{12,4},{... | collective-permute-start | bytes 589832 | tf_op jit(solution)/shard_map/ppermute | solution.py:341
